TPU v7x, 32 devices: a whole 2x2x4 slice. The times are simulated.
32 devices in a mesh: row: 2 (over core), col: 4 (over y, x), depth: 4 (over z).
Axes of the slice: x: 2, y: 2, z: 4, core: 2. Of those that a mesh axis runs over, the one named last changes fastest.
Arguments:
- blocks: float32 [512, 4, 4, 128, 128], P(('row', 'depth'), 'col'), may hold values from -0.9 to 0.9
- columns: int32 [512, 4, 4], P(('row', 'depth'), 'col'), may hold values from 0 to 127, as said below
- counts: int32 [512, 4], P(('row', 'depth'), 'col'), may hold values from 0 to 4, as said below
Outputs:
- purified: float32 [8, 4, 4, 128, 128], P(('row', 'depth'), 'col')
Inputs may be any that keep to these rules, and one draw needn't show every extreme that they name: `columns`: the first counts[i, p] slots of block row i in panel p name distinct places; the panel that holds block column i names it in slot 0. `counts`: the panel that holds block column i has a count of 1 or more.
All inputs are finite; a program needn't handle non-finite values.
Results may differ from a plain program's by a relative error of at most 0.0003.
Values sent between devices are 32-bit elements; how exact they have to be, the bound alone decides.
A program may use at most 128 MiB of HBM per device.

v0:
```python
import jax
import jax.numpy as jnp
from jax import lax
from jax.sharding import PartitionSpec as P

ROWS_WIN = 1


def broadcast(value, axis, root):
    mine = lax.axis_index(axis) == root
    return lax.psum(jnp.where(mine, value, jnp.zeros_like(value)), axis)


def tile_product(
    left_side, left_cols, left_count, out_cols, out_count, inner_blocks, inner_cols, inner_count
):
    slot_ids = jnp.arange(left_cols.shape[-1], dtype=jnp.int32)
    left_valid = slot_ids[None, :] < left_count[:, None]
    taken_blocks = inner_blocks[left_cols]
    taken_cols = inner_cols[left_cols]
    taken_valid = slot_ids < inner_count[left_cols][..., None]
    out_valid = slot_ids < out_count[..., None]
    matched = (taken_cols[..., None] == out_cols[:, None, :, None, :]) & taken_valid[..., None]
    matched = matched & out_valid[:, None, :, None, :] & left_valid[:, :, None, None, None]
    select = jnp.einsum(
        "raqts,raqtyz->raqsyz",
        matched.astype(jnp.float32),
        taken_blocks,
        precision=lax.Precision.HIGHEST,
    )
    return jnp.einsum("raxy,raqsyz->rqsxz", left_side, select, precision=lax.Precision.HIGHEST)


def body(blocks, columns, counts):
    depth_pos = lax.axis_index("depth")
    local_panels = blocks.shape[1]
    panel_pick = depth_pos % local_panels
    owner_col = depth_pos // local_panels
    row_blocks, row_cols, row_count = (
        lax.all_gather(blocks[:ROWS_WIN], "depth", axis=0, tiled=True),
        lax.all_gather(columns[:ROWS_WIN], "depth", axis=0, tiled=True),
        lax.all_gather(counts[:ROWS_WIN], "depth", axis=0, tiled=True),
    )
    pick_blocks = lax.dynamic_index_in_dim(row_blocks, panel_pick, 1, keepdims=False)
    pick_cols = lax.dynamic_index_in_dim(row_cols, panel_pick, 1, keepdims=False)
    pick_count = lax.dynamic_index_in_dim(row_count, panel_pick, 1, keepdims=False)
    left_blocks, left_cols, left_count = (
        broadcast(pick_blocks, "col", owner_col),
        broadcast(pick_cols, "col", owner_col),
        broadcast(pick_count, "col", owner_col),
    )
    inner_blocks, inner_cols, inner_count = (
        lax.all_gather(blocks, "row", axis=0, tiled=True),
        lax.all_gather(columns, "row", axis=0, tiled=True),
        lax.all_gather(counts, "row", axis=0, tiled=True),
    )
    partial_value = tile_product(
        left_blocks,
        left_cols,
        left_count,
        row_cols,
        row_count,
        inner_blocks,
        inner_cols,
        inner_count,
    )
    square_rows = lax.psum(partial_value, "depth")
    square = lax.dynamic_slice_in_dim(square_rows, depth_pos * ROWS_WIN, ROWS_WIN, 0)
    square_panel = lax.dynamic_index_in_dim(square_rows, panel_pick, 1, keepdims=False)
    left_square = broadcast(square_panel, "col", owner_col)
    cube_terms = tile_product(
        left_square,
        left_cols,
        left_count,
        row_cols,
        row_count,
        inner_blocks,
        inner_cols,
        inner_count,
    )
    cube_part = lax.psum_scatter(cube_terms, "depth", scatter_dimension=0, tiled=True)
    return 3.0 * square - 2.0 * cube_part


def solution(mesh):
    placed = (
        P(("row", "depth"), "col", None, None, None),
        P(("row", "depth"), "col", None),
        P(("row", "depth"), "col"),
    )
    return jax.shard_map(
        body,
        mesh=mesh,
        in_specs=placed,
        out_specs=P(("row", "depth"), "col", None, None, None),
        check_vma=False,
    )
```

profile of v0, /device:TPU:0, one launch (start us, length us, event | category | flops | bytes accessed | tf_op | source)
XLA Modules:
  0.0 307.6 jit_solution(15464045596741560751)
XLA Ops:
  6.5 1.7 slice.11
  8.3 0.7 all-gather.3.cloned.1.call-update
  9.1 0.6 dynamic-slice.1
  9.7 0.6 bitcast_dynamic-update-slice_fusion
  10.4 9.9 %all-reduce.1 = s32[4]{0:T(128)S(1)} all-reduce(s32[4]{0:T(128)S(1)} %bitcast_dynamic-update-slice_fusion), channel_id=1, replica_groups=mesh['row'=2,'col'=4,'depth'=4] {'depth'}, use_global_device_ids=true, to_apply=%add.1 | all-reduce | flops 4 | bytes 32 | tf_op jit(solution)/shard_map/lt | solution.py:22
  20.3 9.2 %all_gather.19 = s32[4,1,4]{2,1,0:T(1,128)S(1)} all-gather(s32[1,1,4]{2,1,0:T(1,128)S(1)} %copy.45), channel_id=1, replica_groups=mesh['row'=2,'col'=4,'depth'=4] {'depth'}, dimensions={0}, use_global_device_ids=true | all-gather | bytes 80 | tf_op jit(solution)/shard_map/all_gather | solution.py:41
  29.5 7.3 %all-reduce.2 = (s32[4,4]{1,0:T(4,128)S(1)}, s32[4]{0:T(128)S(1)}) all-reduce(s32[4,4]{1,0:T(4,128)S(1)} %broadcast_select_fusion, s32[4]{0:T(128)S(1)} %broadcast_select_fusion.1), channel_id=1, replica_groups=mesh['row'=2,'col'=4,'depth'=4] {'col'}, use_global_device_ids=true, to_apply=%region_0.1 | all-reduce | flops 20 | bytes 160 | tf_op jit(solution)/shard_map/psum | solution.py:11
  36.9 0.6 dynamic-slice
  38.2 1.8 all-reduce
  40.0 0.7 gather_fusion.1
  40.8 1.9 all_gather.18
  43.2 2.3 fusion.4
  45.8 46.2 %all-gather.3.cloned.1.call-done = f32[128,1,4,128,128]{4,3,2,1,0:T(8,128)} async-done(((f32[64,1,4,128,128]{4,3,2,1,0:T(8,128)}), f32[128,1,4,128,128]{4,3,2,1,0:T(8,128)}) %all-gather.3.cloned.1.call-update) | async-done | bytes 33554448 | tf_op jit(solution)/shard_map/all_gather | solution.py:53
  92.0 5.0 %gather_fusion.2 = f32[16,4,128,128]{3,2,1,0:T(8,128)} fusion(f32[128,4,128,128]{3,2,1,0:T(8,128)} %bitcast.51, s32[1024]{0:T(1024)S(1)} %pad_clamp_fusion), kind=kCustom, calls=%fused_computation.2 | custom fusion | bytes 8388672 | tf_op jit(solution)/shard_map/gather | solution.py:19
  97.0 10.5 %fusion = f32[4,4,4,128,128]{4,2,3,1,0:T(4,128)} fusion(f32[4,4,4,128,128]{4,3,2,1,0:T(8,128)} %bitcast.50, s32[4,4]{1,0:T(4,128)S(1)} %bitcast.55, s32[4,4,4]{2,1,0:T(4,128)S(1)} %bitcast.53, pred[4,4]{1,0:T(4,128)(4,1)S(1)} %iota_compare_fusion.1, pred[4,4]{1,0:T(4,128)(4,1)S(1)} %iota_compare_fusion.2, pred[4,4,4]{2,1,0:T(4,128)(4,1)S(1)} %iota_compare_fusion), kind=kOutput, calls=%fused_computation.3 | convolution fusion | flops 50332672 | bytes 8389024 | tf_op jit(solution)/shard_map/raqts,raqtyz->raqsyz/dot_general | solution.py:25
  107.5 5.3 %copy.32 = f32[4,4,4,128,128]{3,4,1,2,0:T(8,128)} copy(f32[4,4,4,128,128]{4,2,3,1,0:T(4,128)} %fusion) | data formatting | bytes 8388608 | tf_op jit(solution)/shard_map/raqts,raqtyz->raqsyz/dot_general | solution.py:25
  112.7 36.0 %all-reduce.7.cloned.1.call-done = f32[4,4,128,128]{3,2,1,0:T(8,128)} async-done(((f32[4,4,128,128]{3,2,1,0:T(8,128)}), f32[4,4,128,128]{3,2,1,0:T(8,128)}) %all-reduce.7.cloned.1.call-update) | async-done | bytes 1048592 | tf_op jit(solution)/shard_map/psum | solution.py:11
  148.8 7.9 %convolution_bitcast_fusion.1 = f32[4,1,4,128,128]{4,3,2,0,1:T(8,128)} fusion(f32[4,4,4,128,128]{3,4,1,2,0:T(8,128)} %copy.32, f32[4,4,128,128]{3,2,1,0:T(8,128)} %all-reduce.7.cloned.1.call-done), kind=kOutput, calls=%fused_computation.6 | convolution fusion | flops 1610612736 | bytes 6291456 | tf_op jit(solution)/shard_map/raxy,raqsyz->rqsxz/dot_general | solution.py:31
  156.7 51.9 %all-reduce.9.cloned.1.call-done = f32[4,1,4,128,128]{4,3,2,0,1:T(8,128)} async-done(((f32[4,1,4,128,128]{4,3,2,0,1:T(8,128)}), f32[4,1,4,128,128]{4,3,2,0,1:T(8,128)}) %all-reduce.9.cloned.1.call-update) | async-done | bytes 1048592 | tf_op jit(solution)/shard_map/psum | solution.py:67
  208.6 2.3 select_bitcast_fusion
  211.2 52.6 %all-reduce.11.cloned.1.call-done = f32[4,4,128,128]{3,2,1,0:T(8,128)} async-done(((f32[4,4,128,128]{3,2,1,0:T(8,128)}), f32[4,4,128,128]{3,2,1,0:T(8,128)}) %all-reduce.11.cloned.1.call-update) | async-done | bytes 1048592 | tf_op jit(solution)/shard_map/psum | solution.py:11
  263.8 7.9 %convolution_bitcast_fusion = f32[4,1,4,128,128]{4,3,2,0,1:T(8,128)} fusion(f32[4,4,4,128,128]{3,4,1,2,0:T(8,128)} %copy.32, f32[4,4,128,128]{3,2,1,0:T(8,128)} %all-reduce.11.cloned.1.call-done), kind=kOutput, calls=%fused_computation.5 | convolution fusion | flops 1610612736 | bytes 6291456 | tf_op jit(solution)/shard_map/raxy,raqsyz->rqsxz/dot_general | solution.py:31
  271.7 27.3 %reduce-scatter.2.cloned.1.call-done = f32[1,1,4,128,128]{4,3,2,0,1:T(8,128)} async-done(((f32[4,1,4,128,128]{4,3,2,0,1:T(8,128)}), f32[1,1,4,128,128]{4,3,2,0,1:T(8,128)}) %reduce-scatter.2.cloned.1.call-update) | async-done | bytes 262160 | tf_op jit(solution)/shard_map/reduce_scatter | solution.py:81
  299.0 1.8 subtract_bitcast_fusion
  (35 shorter events, 1.8 us)
Async XLA Ops:
  6.5 36.7 %all-gather.5.cloned.1.call-start = ((), (), s32[]{:S(2)}) async-start(), calls=%async_computation.2 | async-start | bytes 1310720 | tf_op jit(solution)/shard_map/all_gather | solution.py:40
  8.2 0.9 copy-start.3
  8.2 1.4 copy-start.1
  8.3 2.0 copy-start
  8.3 28.6 %copy-start.2 = (u32[32]{0:T(128)S(1)}, u32[32]{0:T(128)}, u32[]{:S(2)}) copy-start(u32[32]{0:T(128)} %constant.58) | copy-start | bytes 388
  8.3 83.7 %all-gather.3.cloned.1.call-start = ((), (), s32[]{:S(2)}) async-start(), calls=%async_computation.1 | async-start | bytes 50331648 | tf_op jit(solution)/shard_map/all_gather | solution.py:53
  9.0 139.7 %all-reduce.7.cloned.1.call-start = ((), (), s32[]{:S(2)}) async-start(), calls=%async_computation.3 | async-start | bytes 2097152 | tf_op jit(solution)/shard_map/psum | solution.py:11
  45.5 163.1 %all-reduce.9.cloned.1.call-start = ((), (), s32[]{:S(2)}) async-start(), calls=%async_computation.4 | async-start | bytes 2097152 | tf_op jit(solution)/shard_map/psum | solution.py:67
  156.6 107.2 %all-reduce.11.cloned.1.call-start = ((), (), s32[]{:S(2)}) async-start(), calls=%async_computation.5 | async-start | bytes 2097152 | tf_op jit(solution)/shard_map/psum | solution.py:11
  211.0 88.0 %reduce-scatter.2.cloned.1.call-start = ((), (), s32[]{:S(2)}) async-start(), calls=%async_computation.6 | async-start | bytes 1310720 | tf_op jit(solution)/shard_map/reduce_scatter | solution.py:81
Sparse Core Ops, SparseCore 0:
  8.9 30.6 all-gather.4
  41.2 50.7 all-gather.2
  95.0 53.6 all-reduce.6
  156.8 51.8 all-reduce.8
  211.8 51.9 all-reduce.10
  271.8 27.1 reduce-scatter.1
where the time goes:
time: 308 us
  waiting for transfers between devices  215 us (70%)
  blocking collectives  30 us (10%)
  matrix products  26.2 us (9%)
  local copies, waits for them, and re-layouts  15.4 us (5%)
  between operations  14.1 us (5%)
  other arithmetic  6.61 us (2%)
    psum x2, waiting for transfers between devices, broadcast(): return lax.psum(jnp.where(mine, value, jnp.zeros_like(value)), axis)  88.6 us
    psum x1, waiting for transfers between devices, body(): square_rows = lax.psum(partial_value, 'depth')  51.9 us
    all_gather x1, waiting for transfers between devices, body(): lax.all_gather(blocks, 'row', axis=0, tiled=True)  46.2 us
    reduce_scatter x1, waiting for transfers between devices, body(): lax.psum_scatter(cube_terms, 'depth', scatter_dimension=0, tiled=True)  27.3 us
    dot_general x2, matrix products, tile_product(): jnp.einsum('raxy,raqsyz->rqsxz', left_side, select, precision=lax.Precisi...  15.7 us
    dot_general x1, matrix products, tile_product(): jnp.einsum('raqts,raqtyz->raqsyz', matched.astype(jnp.float32), taken_blo...  10.5 us
    lt x1, blocking collectives, tile_product(): out_valid = slot_ids < out_count[..., None]  9.89 us
    all_gather x1, blocking collectives, body(): lax.all_gather(columns[:ROWS_WIN], 'depth', axis=0, tiled=True)  9.19 us
  transfers between devices with their start and end apart: 6, of which 5 were waited for; matrix products, arithmetic and copies ran while one was open for 9% of the time, Pallas kernels for 0%

commit v1 on v0

v1 whole, which is shorter than its diff:
```python
import functools

import jax
import jax.numpy as jnp
from jax import lax
from jax.experimental import pallas as pl
from jax.experimental.pallas import tpu as pltpu
from jax.sharding import PartitionSpec as P

MESH = pl.DeviceIdType.MESH
LANES = 128
SHORT = 2
SHORT_DIAG = 6
HEAD = 2


def position():
    return lax.axis_index("row"), lax.axis_index("col"), lax.axis_index("depth")


def meta_kernel(rows, cols, depths, meta_ref, all_ref, send_sem, recv_sem, own_sem):
    r, c, d = position()
    devices = rows * cols * depths
    me = (r * depths + d) * cols + c

    def target(other):
        q = other // cols
        return (q // depths, other % cols, q % depths)

    barrier = pltpu.get_barrier_semaphore()

    @pl.loop(1, devices)
    def _(off):
        pl.semaphore_signal(barrier, inc=1, device_id=target((me + off) % devices), device_id_type=MESH)

    own = pltpu.make_async_copy(meta_ref, all_ref.at[me], own_sem)
    own.start()
    pl.semaphore_wait(barrier, devices - 1)

    def copy(slot, other):
        return pltpu.make_async_remote_copy(
            src_ref=meta_ref,
            dst_ref=all_ref.at[slot],
            send_sem=send_sem.at[other],
            recv_sem=recv_sem.at[slot],
            device_id=target(other),
            device_id_type=MESH,
        )

    @pl.loop(1, devices)
    def _(off):
        copy(me, (me + off) % devices).start()

    own.wait()

    @pl.loop(1, devices)
    def _(off):
        other = (me + off) % devices
        copy(other, other).wait_recv()
        copy(me, other).wait_send()


def gather_meta(meta, sizes):
    devices = sizes[0] * sizes[1] * sizes[2]
    return pl.pallas_call(
        functools.partial(meta_kernel, *sizes),
        out_shape=jax.ShapeDtypeStruct((devices, 1, LANES), jnp.int32),
        in_specs=[pl.BlockSpec(memory_space=pltpu.VMEM)],
        out_specs=pl.BlockSpec(memory_space=pltpu.VMEM),
        scratch_shapes=[
            pltpu.SemaphoreType.DMA((devices,)),
            pltpu.SemaphoreType.DMA((devices,)),
            pltpu.SemaphoreType.DMA,
        ],
        compiler_params=pltpu.CompilerParams(collective_id=0, has_side_effects=True),
    )(meta)


def pack_kernel(sizes, dims, win_ref, cols_ref, blocks_ref, pack_ref, codes_ref, sems):
    rows, cols, depths = sizes
    local_rows, panels, slots = dims
    window = rows * depths
    most = slots * slots * panels
    r, c, d = position()
    me_q = r * depths + d
    owner = d // panels
    left_panel = d % panels
    diag = owner == c
    limit = jnp.where(diag, min(SHORT_DIAG, most), min(SHORT, most))
    counts_at = local_rows * panels * slots

    def entry(q, n, row, panel, slot):
        return pltpu.make_async_copy(
            blocks_ref.at[row, panel, slot], pack_ref.at[q, n], sems.at[q]
        )

    def pack_row(q, too_long):
        left_at = q * cols + owner
        out_at = q * cols + c
        left_count = win_ref[left_at, panels * slots + left_panel]

        def left_step(a, n):
            place = win_ref[left_at, left_panel * slots + a]
            row = place % local_rows

            def panel_step(panel, n):
                out_count = win_ref[out_at, panels * slots + panel]
                inner_count = cols_ref[counts_at + row * panels + panel]

                def inner_step(t, n):
                    column = cols_ref[(row * panels + panel) * slots + t]

                    def out_step(s, n):
                        hit = win_ref[out_at, panel * slots + s] == column

                        @pl.when(hit)
                        def _():
                            entry(q, n, row, panel, t).start()
                            codes_ref[q, 0, HEAD + n] = a * (panels * slots) + panel * slots + s

                        return n + hit.astype(jnp.int32)

                    return lax.fori_loop(0, out_count, out_step, n)

                return lax.fori_loop(0, inner_count, inner_step, n)

            mine = place // local_rows == r
            return lax.fori_loop(0, jnp.where(mine, panels, 0), panel_step, n)

        n = lax.fori_loop(0, left_count, left_step, jnp.int32(0))
        codes_ref[q, 0, 0] = n
        return too_long | ((n > limit) & (q != me_q)).astype(jnp.int32)

    too_long = lax.fori_loop(0, window, pack_row, jnp.int32(0))

    @pl.loop(0, window)
    def _(q):
        codes_ref[q, 0, 1] = too_long

        @pl.loop(0, codes_ref[q, 0, 0])
        def _(n):
            entry(q, 0, 0, 0, 0).wait()


def pack_lists(win, cols, blocks, sizes):
    local_rows, panels, slots, size, _ = blocks.shape
    window = sizes[0] * sizes[2]
    most = slots * slots * panels
    return pl.pallas_call(
        functools.partial(pack_kernel, sizes, (local_rows, panels, slots)),
        out_shape=(
            jax.ShapeDtypeStruct((window, most, size, size), jnp.float32),
            jax.ShapeDtypeStruct((window, 1, LANES), jnp.int32),
        ),
        in_specs=[
            pl.BlockSpec(memory_space=pltpu.SMEM),
            pl.BlockSpec(memory_space=pltpu.SMEM),
            pl.BlockSpec(memory_space=pl.ANY),
        ],
        out_specs=(pl.BlockSpec(memory_space=pl.ANY), pl.BlockSpec(memory_space=pltpu.SMEM)),
        scratch_shapes=[pltpu.SemaphoreType.DMA((window,))],
    )(win, cols, blocks)


def exchange_kernel(
    sizes, panels, short, short_diag, pack_ref, codes_ref, left_ref,
    got_ref, got_codes_ref, lefts_ref,
    send_sem, recv_sem, left_send, left_recv, own_sem,
):
    rows, cols, depths = sizes
    window = rows * depths
    most = pack_ref.shape[1]
    r, c, d = position()
    me = r * depths + d

    barrier = pltpu.get_barrier_semaphore()

    @pl.loop(1, window)
    def _(off):
        q = (me + off) % window
        pl.semaphore_signal(barrier, inc=1, device_id=(q // depths, c, q % depths), device_id_type=MESH)

    @pl.loop(1, cols)
    def _(off):
        pl.semaphore_signal(barrier, inc=1, device_id=(r, (c + off) % cols, d), device_id_type=MESH)

    own = [
        pltpu.make_async_copy(pack_ref.at[me], got_ref.at[me], own_sem.at[0]),
        pltpu.make_async_copy(codes_ref.at[me], got_codes_ref.at[me], own_sem.at[1]),
        pltpu.make_async_copy(left_ref, lefts_ref.at[c], own_sem.at[2]),
    ]
    for copy in own:
        copy.start()
    pl.semaphore_wait(barrier, window - 1 + cols - 1)

    def left_copy(slot, other):
        return pltpu.make_async_remote_copy(
            src_ref=left_ref,
            dst_ref=lefts_ref.at[slot],
            send_sem=left_send.at[other],
            recv_sem=left_recv.at[slot],
            device_id=(r, other, d),
            device_id_type=MESH,
        )

    def list_copy(kind, slot, other):
        if kind == 0:
            src, dst = codes_ref.at[other], got_codes_ref.at[slot]
        elif kind == 1:
            src = pack_ref.at[other, pl.ds(0, short)]
            dst = got_ref.at[slot, pl.ds(0, short)]
        else:
            src = pack_ref.at[other, pl.ds(short, short_diag - short)]
            dst = got_ref.at[slot, pl.ds(short, short_diag - short)]
        return pltpu.make_async_remote_copy(
            src_ref=src,
            dst_ref=dst,
            send_sem=send_sem.at[kind, other],
            recv_sem=recv_sem.at[kind, slot],
            device_id=(other // depths, c, other % depths),
            device_id_type=MESH,
        )

    @pl.loop(1, cols)
    def _(off):
        left_copy(c, (c + off) % cols).start()

    @pl.loop(1, window)
    def _(off):
        other = (me + off) % window
        list_copy(0, me, other).start()
        list_copy(1, me, other).start()
        if short_diag > short:
            @pl.when(d // panels == c)
            def _():
                list_copy(2, me, other).start()

    for copy in own:
        copy.wait()

    @pl.loop(1, cols)
    def _(off):
        other = (c + off) % cols
        left_copy(other, other).wait_recv()
        left_copy(c, other).wait_send()

    @pl.loop(1, window)
    def _(off):
        other = (me + off) % window
        list_copy(0, other, other).wait_recv()
        list_copy(0, me, other).wait_send()
        list_copy(1, other, other).wait_recv()
        list_copy(1, me, other).wait_send()
        if short_diag > short:
            @pl.when((other % depths) // panels == c)
            def _():
                list_copy(2, other, other).wait_recv()

            @pl.when(d // panels == c)
            def _():
                list_copy(2, me, other).wait_send()


def exchange(pack, codes, left, sizes, panels, short, short_diag, ident):
    window, most, size, _ = pack.shape
    cols = sizes[1]
    anywhere = pl.BlockSpec(memory_space=pl.ANY)
    return pl.pallas_call(
        functools.partial(exchange_kernel, sizes, panels, min(short, most), min(short_diag, most)),
        out_shape=(
            jax.ShapeDtypeStruct(pack.shape, jnp.float32),
            jax.ShapeDtypeStruct(codes.shape, jnp.int32),
            jax.ShapeDtypeStruct((cols,) + left.shape, jnp.float32),
        ),
        in_specs=[anywhere] * 3,
        out_specs=(anywhere,) * 3,
        scratch_shapes=[
            pltpu.SemaphoreType.DMA((3, window)),
            pltpu.SemaphoreType.DMA((3, window)),
            pltpu.SemaphoreType.DMA((cols,)),
            pltpu.SemaphoreType.DMA((cols,)),
            pltpu.SemaphoreType.DMA((3,)),
        ],
        compiler_params=pltpu.CompilerParams(collective_id=ident, has_side_effects=True),
    )(pack, codes, left)


def multiply_into(acc_ref, lefts_ref, got_ref, codes_ref, held, sems, depths, slots):
    window, most = got_ref.shape[:2]
    out_slots = acc_ref.shape[0]

    def fetch(q, n):
        return pltpu.make_async_copy(got_ref.at[q, n], held.at[q, n], sems.at[q, n])

    @pl.loop(0, window)
    def _(q):
        @pl.loop(0, codes_ref[q, 0, 0])
        def _(n):
            fetch(q, n).start()

    acc_ref[...] = jnp.zeros_like(acc_ref)

    @pl.loop(0, window)
    def _(q):
        @pl.loop(0, codes_ref[q, 0, 0])
        def _(n):
            fetch(q, n).wait()
            code = codes_ref[q, 0, HEAD + n]
            place = (q % depths) * slots + code // out_slots
            s = code % out_slots
            acc_ref[s] += jnp.dot(
                lefts_ref[place],
                held[q, n],
                precision=lax.Precision.HIGHEST,
                preferred_element_type=jnp.float32,
            )


def square_kernel(depths, slots, codes_ref, got_ref, lefts_ref, out_ref, flag_ref, held, sems):
    window = got_ref.shape[0]

    flag_ref[0, 0] = lax.fori_loop(
        0, window, lambda q, f: f | codes_ref[q, 0, 1], jnp.int32(0)
    )
    multiply_into(out_ref, lefts_ref, got_ref, codes_ref, held, sems, depths, slots)


def cube_kernel(depths, slots, codes_ref, got_ref, lefts_ref, square_ref, out_ref, held, sems):
    multiply_into(out_ref, lefts_ref, got_ref, codes_ref, held, sems, depths, slots)
    out_ref[...] = 3.0 * square_ref[...] - 2.0 * out_ref[...]


def local_product(kernel, codes, got, lefts, extra, out_shape, out_specs):
    vmem = pl.BlockSpec(memory_space=pltpu.VMEM)
    return pl.pallas_call(
        kernel,
        out_shape=out_shape,
        in_specs=[
            pl.BlockSpec(memory_space=pltpu.SMEM),
            pl.BlockSpec(memory_space=pl.ANY),
            vmem,
        ] + [vmem] * len(extra),
        out_specs=out_specs,
        scratch_shapes=[
            pltpu.VMEM(got.shape, jnp.float32),
            pltpu.SemaphoreType.DMA(got.shape[:2]),
        ],
        compiler_params=pltpu.CompilerParams(vmem_limit_bytes=32 << 20),
    )(codes, got, lefts, *extra)


def gather_kernel(cols, square_ref, flag_ref, squares_ref, flags_ref, send_sem, recv_sem, own_sem):
    r, c, d = position()
    barrier = pltpu.get_barrier_semaphore()

    @pl.loop(1, cols)
    def _(off):
        pl.semaphore_signal(barrier, inc=1, device_id=(r, (c + off) % cols, d), device_id_type=MESH)

    pairs = ((square_ref, squares_ref), (flag_ref, flags_ref))
    own = [
        pltpu.make_async_copy(src, dst.at[c], own_sem.at[i]) for i, (src, dst) in enumerate(pairs)
    ]
    for copy in own:
        copy.start()
    pl.semaphore_wait(barrier, cols - 1)

    def copies(slot, other):
        return [
            pltpu.make_async_remote_copy(
                src_ref=src,
                dst_ref=dst.at[slot],
                send_sem=send_sem.at[i, other],
                recv_sem=recv_sem.at[i, slot],
                device_id=(r, other, d),
                device_id_type=MESH,
            )
            for i, (src, dst) in enumerate(pairs)
        ]

    @pl.loop(1, cols)
    def _(off):
        for copy in copies(c, (c + off) % cols):
            copy.start()

    for copy in own:
        copy.wait()

    @pl.loop(1, cols)
    def _(off):
        other = (c + off) % cols
        for copy in copies(other, other):
            copy.wait_recv()
        for copy in copies(c, other):
            copy.wait_send()


def gather_square(square, flag, cols, ident):
    anywhere = pl.BlockSpec(memory_space=pl.ANY)
    return pl.pallas_call(
        functools.partial(gather_kernel, cols),
        out_shape=(
            jax.ShapeDtypeStruct((cols,) + square.shape, jnp.float32),
            jax.ShapeDtypeStruct((cols,) + flag.shape, jnp.int32),
        ),
        in_specs=[anywhere] * 2,
        out_specs=(anywhere,) * 2,
        scratch_shapes=[
            pltpu.SemaphoreType.DMA((2, cols)),
            pltpu.SemaphoreType.DMA((2, cols)),
            pltpu.SemaphoreType.DMA((2,)),
        ],
        compiler_params=pltpu.CompilerParams(collective_id=ident, has_side_effects=True),
    )(square, flag)


def body(sizes, blocks, columns, counts):
    rows, cols, depths = sizes
    local_rows, panels, slots, size, _ = blocks.shape
    most = slots * slots * panels
    out_slots = panels * slots
    meta = jnp.concatenate([columns[0].reshape(-1), counts[0].reshape(-1)])
    meta = jnp.pad(meta, (0, LANES - meta.shape[0]))[None, :]
    win = gather_meta(meta, sizes)[:, 0, :]
    local = jnp.concatenate([columns.reshape(-1), counts.reshape(-1)])
    pack, codes = pack_lists(win, local, blocks, sizes)
    left = blocks[0].reshape(out_slots, size, size)
    block_shape = jax.ShapeDtypeStruct((out_slots, size, size), jnp.float32)
    vmem = pl.BlockSpec(memory_space=pltpu.VMEM)

    def square_step(short, short_diag, ident):
        got, got_codes, lefts = exchange(
            pack, codes, left, sizes, panels, short, short_diag, ident
        )
        room = jnp.full((rows, depths), min(short, most), jnp.int32)
        at = jnp.arange(depths, dtype=jnp.int32)[None, :] // panels == lax.axis_index("col")
        room = jnp.where(at, min(short_diag, most), room)
        is_me = (jnp.arange(rows)[:, None] == lax.axis_index("row")) & (
            jnp.arange(depths)[None, :] == lax.axis_index("depth")
        )
        room = jnp.where(is_me, most, room).reshape(-1, 1, 1)
        head = jnp.arange(LANES)[None, None, :] == 0
        got_codes = jnp.where(head, jnp.minimum(got_codes, room), got_codes)
        square, flag = local_product(
            functools.partial(square_kernel, depths, slots),
            got_codes, got, lefts.reshape(cols * out_slots, size, size), (),
            (block_shape, jax.ShapeDtypeStruct((1, LANES), jnp.int32)),
            (vmem, pl.BlockSpec(memory_space=pltpu.SMEM)),
        )
        squares, flags = gather_square(square, flag, cols, ident + 1)
        return got, got_codes, square, squares, flags

    def cube_step(got, got_codes, square, squares):
        return local_product(
            functools.partial(cube_kernel, depths, slots),
            got_codes, got, squares.reshape(cols * out_slots, size, size), (square,),
            block_shape, vmem,
        )

    got, got_codes, square, squares, flags = square_step(SHORT, SHORT_DIAG, 1)
    too_long = jnp.any(flags[:, 0, 0] != 0)

    def again():
        got, got_codes, square, squares, _ = square_step(most, most, 3)
        return cube_step(got, got_codes, square, squares)

    out = lax.cond(
        too_long, again, lambda: cube_step(got, got_codes, square, squares)
    )
    return out.reshape(1, panels, slots, size, size)


def solution(mesh):
    placed = (
        P(("row", "depth"), "col", None, None, None),
        P(("row", "depth"), "col", None),
        P(("row", "depth"), "col"),
    )
    sizes = (mesh.shape["row"], mesh.shape["col"], mesh.shape["depth"])
    return jax.shard_map(
        functools.partial(body, sizes),
        mesh=mesh,
        in_specs=placed,
        out_specs=P(("row", "depth"), "col", None, None, None),
        check_vma=False,
    )
```

time: 308 us -> 129 us (0.42)
  the two profiles are of different devices: /device:TPU:0 before, /device:TPU:8 now
where the time goes in v1:
time: 129 us; the launch traced here: 127 us
  Pallas kernels  117 us (91%)
  local copies, waits for them, and re-layouts  5.66 us (4%)
  other arithmetic  4.12 us (3%)
    pallas_call x1, Pallas kernels, exchange(): pl.pallas_call(functools.partial(exchange_kernel, sizes, panels, min(shor...  50 us
    pallas_call x1, Pallas kernels, gather_square(): pl.pallas_call(functools.partial(gather_kernel, cols), out_shape=(jax.Sha...  40 us
    pallas_call x1, Pallas kernels, gather_meta(): pl.pallas_call(functools.partial(meta_kernel, *sizes), out_shape=jax.Shap...  9.36 us
    pallas_call x1, Pallas kernels, pack_lists(): pl.pallas_call(functools.partial(pack_kernel, sizes, (local_rows, panels,...  8.93 us
    pallas_call x2, Pallas kernels, local_product(): pl.pallas_call(kernel, out_shape=out_shape, in_specs=[pl.BlockSpec(memory...  8.5 us
    unnamed x7, local copies, waits for them, and re-layouts  3.2 us

profile of v1, /device:TPU:8, one launch (start us, length us, event | category | flops | bytes accessed | tf_op | source)
XLA Modules:
  0.0 127.4 jit_solution(9868942326509970073)
XLA Ops:
  0.0 0.1 and_select_fusion
  0.1 0.1 select_n.40
  0.2 0.8 slice_reduce_fusion
  1.0 0.7 pad_add_fusion.1
  1.7 0.5 pad_bitcast_fusion.meta_ref
  2.2 9.4 %shard_map.39 = s32[32,1,128]{2,1,0:T(1,128)} custom-call(s32[1,128]{1,0:T(1,128)} %pad_bitcast_fusion.meta_ref), custom_call_target="tpu_custom_call" | custom-call | tf_op jit(solution)/shard_map/pallas_call | solution.py:65
  11.6 0.8 copy.6
  12.4 0.1 reshape.148
  12.5 1.2 pad_add_fusion.cols_ref
  13.7 1.0 slice_bitcast_fusion.left_ref
  14.7 8.9 %shard_map.40 = (f32[8,16,128,128]{3,2,1,0:T(8,128)}, s32[8,1,128]{2,1,0:T(1,128)S(1)}) custom-call(s32[32,128]{1,0:T(8,128)} %bitcast.22, s32[320]{0:T(512)} %pad_add_fusion.cols_ref, f32[64,1,4,128,128]{4,3,2,1,0:T(8,128)} %blocks_ref.1), custom_call_target="tpu_custom_call" | custom-call | tf_op jit(solution)/shard_map/pallas_call | solution.py:149
  23.6 50.0 %shard_map.41 = (f32[8,16,128,128]{3,2,1,0:T(8,128)}, s32[8,1,128]{2,1,0:T(1,128)}, f32[4,4,128,128]{3,2,1,0:T(8,128)}) custom-call(f32[8,16,128,128]{3,2,1,0:T(8,128)} %get-tuple-element.45.pack_ref, s32[8,1,128]{2,1,0:T(1,128)S(1)} %get-tuple-element.46.codes_ref, f32[4,128,128]{2,1,0:T(8,128)S(1)} %slice_bitcast_fusion.left_ref), custom_call_target="tpu_custom_call" | custom-call | tf_op jit(solution)/shard_map/pallas_call | solution.py:268
  73.6 0.7 broadcast_select_fusion.1.codes_ref
  74.4 0.0 copy-start.2
  74.4 1.2 copy-done.2
  75.6 4.6 %shard_map.42 = (f32[4,128,128]{2,1,0:T(8,128)S(1)}, s32[1,128]{1,0:T(1,128)S(1)}) custom-call(s32[8,1,128]{2,1,0:T(1,128)S(1)} %broadcast_select_fusion.1.codes_ref, f32[8,16,128,128]{3,2,1,0:T(8,128)} %get-tuple-element.48.got_ref, f32[16,128,128]{2,1,0:T(8,128)S(1)} %bitcast.16), custom_call_target="tpu_custom_call" | custom-call | tf_op jit(solution)/shard_map/pallas_call | solution.py:335
  80.2 0.0 copy-start.7
  80.2 0.5 copy-done.7
  80.7 40.0 %shard_map.43 = (f32[4,4,128,128]{3,2,1,0:T(8,128)S(1)}, s32[4,1,128]{2,1,0:T(1,128)}) custom-call(f32[4,128,128]{2,1,0:T(8,128)S(1)} %get-tuple-element.50.square_ref, s32[1,128]{1,0:T(1,128)} %copy-done.7), custom_call_target="tpu_custom_call" | custom-call | tf_op jit(solution)/shard_map/pallas_call | solution.py:400
  120.7 1.3 %compare_reduce_fusion = pred[]{:T(512)} fusion(s32[4,1,128]{2,1,0:T(1,128)} %get-tuple-element.52), kind=kLoop, calls=%fused_computation.3 | loop fusion | flops 7 | bytes 17 | tf_op jit(solution)/shard_map/reduce_or | solution.py:461
  122.7 4.0 %conditional.1 = (f32[1,1,4,128,128]{4,3,2,1,0:T(8,128)S(1)}) conditional(s32[]{:T(128)} %convert_element_type.3, (f32[4,4,128,128]{3,2,1,0:T(8,128)S(1)}, s32[8,1,128]{2,1,0:T(1,128)S(1)}, f32[8,16,128,128]{3,2,1,0:T(8,128)}, f32[4,128,128]{2,1,0:T(8,128)S(1)}) %tuple.13, (f32[8,16,128,128]{3,2,1,0:T(8,128)}, s32[8,1,128]{2,1,0:T(1,128)S(1)}, ...), branch_computations={%region_1.2_spmd, %region_2.3_spmd} | conditional | flops 2176 | bytes 77605344 | solution.py:467
  122.7 3.9 %branch_0_fun.1 = f32[4,128,128]{2,1,0:T(8,128)S(1)} custom-call(s32[8,1,128]{2,1,0:T(1,128)S(1)} %get-tuple-element.23.codes_ref, f32[8,16,128,128]{3,2,1,0:T(8,128)} %get-tuple-element.24.got_ref, f32[16,128,128]{2,1,0:T(8,128)S(1)} %bitcast.19, f32[4,128,128]{2,1,0:T(8,128)S(1)} %get-tuple-element.26.square_ref), custom_call_target="tpu_custom_call" | custom-call | tf_op jit(solution)/shard_map/cond/branch_0_fun/pallas_call | solution.py:335
  126.7 0.0 copy-start.9
  126.7 0.7 copy-done.9
  (4 shorter events, 0.0 us)
Async XLA Ops:
  74.4 1.2 copy-start.2
  80.2 0.5 copy-start.7
  126.7 0.7 copy-start.9

commit v2 on v1

v2 whole, which is shorter than its diff:
```python
import functools

import jax
import jax.numpy as jnp
from jax import lax
from jax.experimental import pallas as pl
from jax.experimental.pallas import tpu as pltpu
from jax.sharding import PartitionSpec as P

MESH = pl.DeviceIdType.MESH
LANES = 128
VMEM_LIMIT = 48 << 20
SHORT = 2
SHORT_DIAG = 6
HEAD = 2
SOURCE = LANES // 2


def position():
    return lax.axis_index("row"), lax.axis_index("col"), lax.axis_index("depth")


def meta_kernel(sizes, panels, local_ref, all_ref, send_sem, recv_sem, own_sem):
    rows, cols, depths = sizes
    window = rows * depths
    r, c, d = position()
    me_q = r * depths + d
    owner = d // panels
    meta_ref = local_ref.at[0]

    def column_mate(off):
        q = (me_q + off) % window
        return q, c

    def inner_mate(i):
        col = (c + 1 + i // (rows * panels)) % cols
        row = (i // panels) % rows
        return row * depths + c * panels + i % panels, col

    def left_source(i):
        return i, owner

    mates = window - 1
    inner = rows * panels * (cols - 1)
    sources = jnp.where(owner == c, 0, window)

    def device(q, col):
        return (q // depths, col, q % depths)

    barrier = pltpu.get_barrier_semaphore()

    def greet(q, col):
        pl.semaphore_signal(barrier, inc=1, device_id=device(q, col), device_id_type=MESH)

    @pl.loop(1, window)
    def _(off):
        greet(*column_mate(off))

    @pl.loop(0, sources)
    def _(i):
        greet(*left_source(i))

    own = pltpu.make_async_copy(meta_ref, all_ref.at[me_q * cols + c], own_sem)
    own.start()
    pl.semaphore_wait(barrier, mates + inner)

    def copy(slot, q, col):
        return pltpu.make_async_remote_copy(
            src_ref=meta_ref,
            dst_ref=all_ref.at[slot],
            send_sem=send_sem.at[q * cols + col],
            recv_sem=recv_sem.at[slot],
            device_id=device(q, col),
            device_id_type=MESH,
        )

    me = me_q * cols + c

    @pl.loop(0, inner)
    def _(i):
        copy(me, *inner_mate(i)).start()

    @pl.loop(1, window)
    def _(off):
        copy(me, *column_mate(off)).start()

    own.wait()

    @pl.loop(1, window)
    def _(off):
        q, col = column_mate(off)
        copy(q * cols + col, q, col).wait_recv()
        copy(me, q, col).wait_send()

    @pl.loop(0, sources)
    def _(i):
        q, col = left_source(i)
        copy(q * cols + col, q, col).wait_recv()

    @pl.loop(0, inner)
    def _(i):
        copy(me, *inner_mate(i)).wait_send()


def gather_meta(local, sizes, panels):
    devices = sizes[0] * sizes[1] * sizes[2]
    return pl.pallas_call(
        functools.partial(meta_kernel, sizes, panels),
        out_shape=jax.ShapeDtypeStruct((devices, 1, LANES), jnp.int32),
        in_specs=[pl.BlockSpec(memory_space=pltpu.VMEM)],
        out_specs=pl.BlockSpec(memory_space=pltpu.VMEM),
        scratch_shapes=[
            pltpu.SemaphoreType.DMA((devices,)),
            pltpu.SemaphoreType.DMA((devices,)),
            pltpu.SemaphoreType.DMA,
        ],
        compiler_params=pltpu.CompilerParams(collective_id=0, has_side_effects=True),
    )(local)


def pack_kernel(sizes, dims, short, win_ref, local_ref, blocks_ref, pack_ref, codes_ref, sem):
    rows, cols, depths = sizes
    local_rows, panels, slots = dims
    window = rows * depths
    capacity = pack_ref.shape[1]
    r, c, d = position()
    me_q = r * depths + d
    owner = d // panels
    left_panel = d % panels
    counts_at = panels * slots
    limit = jnp.where(owner == c, capacity, short)

    def entry(q, n, row, panel, slot):
        return pltpu.make_async_copy(blocks_ref.at[row, panel, slot], pack_ref.at[q, n], sem)

    def pack_row(q, carry):
        too_long, copies = carry
        left_at = q * cols + owner
        out_at = q * cols + c
        left_count = win_ref[left_at, 0, counts_at + left_panel]
        room = jnp.where(q == me_q, 0, limit)

        def left_step(a, n):
            place = win_ref[left_at, 0, left_panel * slots + a]
            row = place % local_rows

            def panel_step(panel, n):
                out_count = win_ref[out_at, 0, counts_at + panel]
                inner_count = local_ref[row, 0, counts_at + panel]

                def inner_step(t, n):
                    column = local_ref[row, 0, panel * slots + t]

                    def out_step(s, n):
                        hit = win_ref[out_at, 0, panel * slots + s] == column

                        @pl.when(hit)
                        def _():
                            codes_ref[q, 0, HEAD + n] = a * counts_at + panel * slots + s
                            codes_ref[q, 0, SOURCE + n] = (row * panels + panel) * slots + t

                        @pl.when(hit & (n < room))
                        def _():
                            entry(q, n, row, panel, t).start()

                        return n + hit.astype(jnp.int32)

                    return lax.fori_loop(0, out_count, out_step, n)

                return lax.fori_loop(0, inner_count, inner_step, n)

            mine = place // local_rows == r
            return lax.fori_loop(0, jnp.where(mine, panels, 0), panel_step, n)

        n = lax.fori_loop(0, left_count, left_step, jnp.int32(0))
        codes_ref[q, 0, 0] = n
        over = ((n > limit) & (q != me_q)).astype(jnp.int32)
        return too_long | over, copies + jnp.minimum(n, room)

    zero = jnp.int32(0)
    too_long, copies = lax.fori_loop(0, window, pack_row, (zero, zero))

    @pl.loop(0, window)
    def _(q):
        codes_ref[q, 0, 1] = too_long

    @pl.loop(0, copies)
    def _(n):
        entry(0, 0, 0, 0, 0).wait()


def pack_lists(win, local, blocks, sizes, short, capacity):
    local_rows, panels, slots, size, _ = blocks.shape
    window = sizes[0] * sizes[2]
    return pl.pallas_call(
        functools.partial(pack_kernel, sizes, (local_rows, panels, slots), short),
        out_shape=(
            jax.ShapeDtypeStruct((window, capacity, size, size), jnp.float32),
            jax.ShapeDtypeStruct((window, 1, LANES), jnp.int32),
        ),
        in_specs=[
            pl.BlockSpec(memory_space=pltpu.SMEM),
            pl.BlockSpec(memory_space=pltpu.SMEM),
            pl.BlockSpec(memory_space=pltpu.HBM),
        ],
        out_specs=(pl.BlockSpec(memory_space=pltpu.VMEM), pl.BlockSpec(memory_space=pltpu.SMEM)),
        scratch_shapes=[pltpu.SemaphoreType.DMA],
        compiler_params=pltpu.CompilerParams(vmem_limit_bytes=VMEM_LIMIT),
    )(win, local, blocks)


def exchange_kernel(
    sizes, panels, short, pack_ref, codes_ref, blocks_ref,
    got_ref, got_codes_ref, lefts_ref,
    send_sem, recv_sem, left_send, left_recv, own_sem,
):
    rows, cols, depths = sizes
    window = rows * depths
    short_diag = pack_ref.shape[1]
    left_ref = blocks_ref.at[0]
    r, c, d = position()
    me = r * depths + d

    barrier = pltpu.get_barrier_semaphore()

    @pl.loop(1, window)
    def _(off):
        q = (me + off) % window
        pl.semaphore_signal(barrier, inc=1, device_id=(q // depths, c, q % depths), device_id_type=MESH)

    @pl.loop(1, cols)
    def _(off):
        pl.semaphore_signal(barrier, inc=1, device_id=(r, (c + off) % cols, d), device_id_type=MESH)

    own = [
        pltpu.make_async_copy(codes_ref.at[me], got_codes_ref.at[me], own_sem.at[0]),
        pltpu.make_async_copy(left_ref, lefts_ref.at[c], own_sem.at[1]),
    ]
    for copy in own:
        copy.start()
    pl.semaphore_wait(barrier, window - 1 + cols - 1)

    def left_copy(slot, other):
        return pltpu.make_async_remote_copy(
            src_ref=left_ref,
            dst_ref=lefts_ref.at[slot],
            send_sem=left_send.at[other],
            recv_sem=left_recv.at[slot],
            device_id=(r, other, d),
            device_id_type=MESH,
        )

    def list_copy(kind, slot, other):
        if kind == 0:
            src, dst = codes_ref.at[other], got_codes_ref.at[slot]
        elif kind == 1:
            src = pack_ref.at[other, pl.ds(0, short)]
            dst = got_ref.at[slot, pl.ds(0, short)]
        else:
            src = pack_ref.at[other, pl.ds(short, short_diag - short)]
            dst = got_ref.at[slot, pl.ds(short, short_diag - short)]
        return pltpu.make_async_remote_copy(
            src_ref=src,
            dst_ref=dst,
            send_sem=send_sem.at[kind, other],
            recv_sem=recv_sem.at[kind, slot],
            device_id=(other // depths, c, other % depths),
            device_id_type=MESH,
        )

    @pl.loop(1, cols)
    def _(off):
        left_copy(c, (c + off) % cols).start()

    @pl.loop(1, window)
    def _(off):
        other = (me + off) % window
        list_copy(0, me, other).start()
        list_copy(1, me, other).start()
        if short_diag > short:
            @pl.when(d // panels == c)
            def _():
                list_copy(2, me, other).start()

    for copy in own:
        copy.wait()

    @pl.loop(1, cols)
    def _(off):
        other = (c + off) % cols
        left_copy(other, other).wait_recv()
        left_copy(c, other).wait_send()

    @pl.loop(1, window)
    def _(off):
        other = (me + off) % window
        list_copy(0, other, other).wait_recv()
        list_copy(0, me, other).wait_send()
        list_copy(1, other, other).wait_recv()
        list_copy(1, me, other).wait_send()
        if short_diag > short:
            @pl.when((other % depths) // panels == c)
            def _():
                list_copy(2, other, other).wait_recv()

            @pl.when(d // panels == c)
            def _():
                list_copy(2, me, other).wait_send()


def exchange(pack, codes, blocks, sizes, short, ident):
    window = pack.shape[0]
    cols = sizes[1]
    panels = blocks.shape[1]
    vmem = pl.BlockSpec(memory_space=pltpu.VMEM)
    return pl.pallas_call(
        functools.partial(exchange_kernel, sizes, panels, short),
        out_shape=(
            jax.ShapeDtypeStruct(pack.shape, jnp.float32),
            jax.ShapeDtypeStruct(codes.shape, jnp.int32),
            jax.ShapeDtypeStruct((cols,) + blocks.shape[1:], jnp.float32),
        ),
        in_specs=[vmem, vmem, pl.BlockSpec(memory_space=pltpu.HBM)],
        out_specs=(vmem,) * 3,
        scratch_shapes=[
            pltpu.SemaphoreType.DMA((3, window)),
            pltpu.SemaphoreType.DMA((3, window)),
            pltpu.SemaphoreType.DMA((cols,)),
            pltpu.SemaphoreType.DMA((cols,)),
            pltpu.SemaphoreType.DMA((2,)),
        ],
        compiler_params=pltpu.CompilerParams(
            collective_id=ident, has_side_effects=True, vmem_limit_bytes=VMEM_LIMIT
        ),
    )(pack, codes, blocks)


def multiply_into(acc_ref, lefts_ref, got_ref, blocks_ref, codes_ref, held, sems, sizes, short):
    rows, cols, depths = sizes
    window, capacity = got_ref.shape[:2]
    panels, slots = blocks_ref.shape[1:3]
    out_slots = panels * slots
    r, c, d = position()
    me_q = r * depths + d
    own = codes_ref[me_q, 0, 0]

    def fetch(n):
        at = codes_ref[me_q, 0, SOURCE + n]
        row = at // out_slots
        block = blocks_ref.at[row, (at // slots) % panels, at % slots]
        return pltpu.make_async_copy(block, held.at[n], sems.at[n])

    @pl.loop(0, own)
    def _(n):
        fetch(n).start()

    acc_ref[...] = jnp.zeros_like(acc_ref)

    def add(q, n, right):
        code = codes_ref[q, 0, HEAD + n]
        depth = q % depths
        left = lefts_ref[depth // panels, depth % panels, code // out_slots]
        s = code % out_slots
        acc_ref[s // slots, s % slots] += jnp.dot(
            left, right, precision=lax.Precision.HIGHEST, preferred_element_type=jnp.float32
        )

    @pl.loop(0, window)
    def _(q):
        room = jnp.where((q % depths) // panels == c, capacity, short)
        room = jnp.where(q == me_q, 0, room)

        @pl.loop(0, jnp.minimum(codes_ref[q, 0, 0], room))
        def _(n):
            add(q, n, got_ref[q, n])

    @pl.loop(0, own)
    def _(n):
        fetch(n).wait()
        add(me_q, n, held[n])


def square_kernel(
    sizes, short, codes_ref, got_ref, blocks_ref, lefts_ref, out_ref, flag_ref, held, sems
):
    flag_ref[0, 0] = lax.fori_loop(
        0, got_ref.shape[0], lambda q, f: f | codes_ref[q, 0, 1], jnp.int32(0)
    )
    multiply_into(out_ref, lefts_ref, got_ref, blocks_ref, codes_ref, held, sems, sizes, short)


def cube_kernel(
    sizes, short, codes_ref, got_ref, blocks_ref, lefts_ref, square_ref, out_ref, held, sems
):
    multiply_into(out_ref, lefts_ref, got_ref, blocks_ref, codes_ref, held, sems, sizes, short)
    out_ref[...] = 3.0 * square_ref[...] - 2.0 * out_ref[...]


def local_product(kernel, codes, got, blocks, lefts, extra, out_shape, out_specs):
    vmem = pl.BlockSpec(memory_space=pltpu.VMEM)
    _, panels, slots, size, _ = blocks.shape
    most = slots * slots * panels
    return pl.pallas_call(
        kernel,
        out_shape=out_shape,
        in_specs=[
            pl.BlockSpec(memory_space=pltpu.SMEM),
            vmem,
            pl.BlockSpec(memory_space=pltpu.HBM),
            vmem,
        ] + [vmem] * len(extra),
        out_specs=out_specs,
        scratch_shapes=[
            pltpu.VMEM((most, size, size), jnp.float32),
            pltpu.SemaphoreType.DMA((most,)),
        ],
        compiler_params=pltpu.CompilerParams(vmem_limit_bytes=VMEM_LIMIT),
    )(codes, got, blocks, lefts, *extra)


def gather_kernel(cols, square_ref, flag_ref, squares_ref, flags_ref, send_sem, recv_sem, own_sem):
    r, c, d = position()
    barrier = pltpu.get_barrier_semaphore()

    @pl.loop(1, cols)
    def _(off):
        pl.semaphore_signal(barrier, inc=1, device_id=(r, (c + off) % cols, d), device_id_type=MESH)

    pairs = ((square_ref, squares_ref), (flag_ref, flags_ref))
    own = [
        pltpu.make_async_copy(src, dst.at[c], own_sem.at[i]) for i, (src, dst) in enumerate(pairs)
    ]
    for copy in own:
        copy.start()
    pl.semaphore_wait(barrier, cols - 1)

    def copies(slot, other):
        return [
            pltpu.make_async_remote_copy(
                src_ref=src,
                dst_ref=dst.at[slot],
                send_sem=send_sem.at[i, other],
                recv_sem=recv_sem.at[i, slot],
                device_id=(r, other, d),
                device_id_type=MESH,
            )
            for i, (src, dst) in enumerate(pairs)
        ]

    @pl.loop(1, cols)
    def _(off):
        for copy in copies(c, (c + off) % cols):
            copy.start()

    for copy in own:
        copy.wait()

    @pl.loop(1, cols)
    def _(off):
        other = (c + off) % cols
        for copy in copies(other, other):
            copy.wait_recv()
        for copy in copies(c, other):
            copy.wait_send()


def gather_square(square, flag, cols, ident):
    vmem = pl.BlockSpec(memory_space=pltpu.VMEM)
    return pl.pallas_call(
        functools.partial(gather_kernel, cols),
        out_shape=(
            jax.ShapeDtypeStruct((cols,) + square.shape, jnp.float32),
            jax.ShapeDtypeStruct((cols,) + flag.shape, jnp.int32),
        ),
        in_specs=[vmem] * 2,
        out_specs=(vmem,) * 2,
        scratch_shapes=[
            pltpu.SemaphoreType.DMA((2, cols)),
            pltpu.SemaphoreType.DMA((2, cols)),
            pltpu.SemaphoreType.DMA((2,)),
        ],
        compiler_params=pltpu.CompilerParams(collective_id=ident, has_side_effects=True),
    )(square, flag)


def body(sizes, blocks, columns, counts):
    rows, cols, depths = sizes
    local_rows, panels, slots, size, _ = blocks.shape
    most = slots * slots * panels
    local = jnp.concatenate([columns.reshape(local_rows, 1, panels * slots), counts[:, None, :]], 2)
    local = jnp.pad(local, ((0, 0), (0, 0), (0, LANES - local.shape[2])))
    win = gather_meta(local, sizes, panels)
    block_shape = jax.ShapeDtypeStruct(blocks.shape[1:], jnp.float32)
    vmem = pl.BlockSpec(memory_space=pltpu.VMEM)

    def square_step(short, capacity, ident):
        pack, codes = pack_lists(win, local, blocks, sizes, short, capacity)
        got, got_codes, lefts = exchange(pack, codes, blocks, sizes, short, ident)
        square, flag = local_product(
            functools.partial(square_kernel, sizes, short),
            got_codes, got, blocks, lefts, (),
            (block_shape, jax.ShapeDtypeStruct((1, LANES), jnp.int32)),
            (vmem, pl.BlockSpec(memory_space=pltpu.SMEM)),
        )
        squares, flags = gather_square(square, flag, cols, ident + 1)
        return got, got_codes, square, squares, flags

    def cube_step(short, got, got_codes, square, squares):
        return local_product(
            functools.partial(cube_kernel, sizes, short),
            got_codes, got, blocks, squares, (square,), block_shape, vmem,
        )

    short = min(SHORT, most)
    *lists, flags = square_step(short, min(SHORT_DIAG, most), 1)

    def again():
        *lists, _ = square_step(most, most, 3)
        return cube_step(most, *lists)

    out = lax.cond(jnp.any(flags[:, 0, 0] != 0), again, lambda: cube_step(short, *lists))
    return out[None]


def solution(mesh):
    placed = (
        P(("row", "depth"), "col", None, None, None),
        P(("row", "depth"), "col", None),
        P(("row", "depth"), "col"),
    )
    sizes = (mesh.shape["row"], mesh.shape["col"], mesh.shape["depth"])
    return jax.shard_map(
        functools.partial(body, sizes),
        mesh=mesh,
        in_specs=placed,
        out_specs=P(("row", "depth"), "col", None, None, None),
        check_vma=False,
    )
```

time: 129 us -> 95.6 us (0.74)
  the two profiles are of different devices: /device:TPU:8 before, /device:TPU:0 now
where the time goes in v2:
time: 95.6 us; the launch traced here: 95.7 us
  Pallas kernels  91.4 us (96%)
  local copies, waits for them, and re-layouts  2.04 us (2%)
  other arithmetic  1.43 us (1%)
    pallas_call x1, Pallas kernels, exchange(): pl.pallas_call(functools.partial(exchange_kernel, sizes, panels, short),...  53.6 us
    pallas_call x1, Pallas kernels, gather_square(): pl.pallas_call(functools.partial(gather_kernel, cols), out_shape=(jax.Sha...  15.2 us
    pallas_call x1, Pallas kernels, gather_meta(): pl.pallas_call(functools.partial(meta_kernel, sizes, panels), out_shape=j...  9.68 us
    pallas_call x2, Pallas kernels, local_product(): pl.pallas_call(kernel, out_shape=out_shape, in_specs=[pl.BlockSpec(memory...  7.28 us
    pallas_call x1, Pallas kernels, pack_lists(): pl.pallas_call(functools.partial(pack_kernel, sizes, (local_rows, panels,...  5.62 us

profile of v2, /device:TPU:0, one launch (start us, length us, event | category | flops | bytes accessed | tf_op | source)
XLA Modules:
  0.0 95.7 jit_solution(9461845830960942952)
XLA Ops:
  0.0 0.8 copy.11
  0.8 0.7 copy.12
  1.5 0.1 pad_add_fusion
  1.7 9.7 %shard_map.39.win_ref = s32[32,1,128]{2,1,0:T(1,128)S(1)} custom-call(s32[64,1,128]{2,1,0:T(1,128)S(1)} %pad.4.local_ref), custom_call_target="tpu_custom_call" | custom-call | tf_op jit(solution)/shard_map/pallas_call | solution.py:107
  11.4 5.6 %shard_map.40 = (f32[8,6,128,128]{3,2,1,0:T(8,128)S(1)}, s32[8,1,128]{2,1,0:T(1,128)S(1)}) custom-call(s32[32,1,128]{2,1,0:T(1,128)S(1)} %shard_map.39.win_ref, s32[64,1,128]{2,1,0:T(1,128)S(1)} %pad.4.local_ref, f32[64,1,4,128,128]{4,3,2,1,0:T(8,128)} %blocks_ref.5), custom_call_target="tpu_custom_call" | custom-call | tf_op jit(solution)/shard_map/pallas_call | solution.py:195
  17.0 53.6 %shard_map.41 = (f32[8,6,128,128]{3,2,1,0:T(8,128)S(1)}, s32[8,1,128]{2,1,0:T(1,128)S(1)}, f32[4,1,4,128,128]{4,3,2,1,0:T(8,128)S(1)}) custom-call(f32[8,6,128,128]{3,2,1,0:T(8,128)S(1)} %get-tuple-element.50.pack_ref, s32[8,1,128]{2,1,0:T(1,128)S(1)} %get-tuple-element.51.codes_ref, f32[64,1,4,128,128]{4,3,2,1,0:T(8,128)} %blocks_ref.5), custom_call_target="tpu_custom_call" | custom-call | tf_op jit(solution)/shard_map/pallas_call | solution.py:316
  70.6 3.3 %shard_map.42 = (f32[1,4,128,128]{3,2,1,0:T(8,128)S(1)}, s32[1,128]{1,0:T(1,128)S(1)}) custom-call(s32[8,1,128]{2,1,0:T(1,128)S(1)} %get-tuple-element.52.codes_ref, f32[8,6,128,128]{3,2,1,0:T(8,128)S(1)} %get-tuple-element.53.got_ref, f32[64,1,4,128,128]{4,3,2,1,0:T(8,128)} %blocks_ref.5, f32[4,1,4,128,128]{4,3,2,1,0:T(8,128)S(1)} %get-tuple-element.54.lefts_ref), custom_call_target="tpu_custom_call" | custom-call | tf_op jit(solution)/shard_map/pallas_call | solution.py:403
  73.9 0.0 copy-start.3
  73.9 0.5 copy-done.3
  74.4 15.2 %shard_map.43 = (f32[4,1,4,128,128]{4,3,2,1,0:T(8,128)}, s32[4,1,128]{2,1,0:T(1,128)}) custom-call(f32[1,4,128,128]{3,2,1,0:T(8,128)S(1)} %get-tuple-element.55.square_ref, s32[1,128]{1,0:T(1,128)} %copy-done.3), custom_call_target="tpu_custom_call" | custom-call | tf_op jit(solution)/shard_map/pallas_call | solution.py:469
  89.7 1.3 %compare_reduce_fusion = pred[]{:T(512)} fusion(s32[4,1,128]{2,1,0:T(1,128)} %get-tuple-element.57), kind=kLoop, calls=%fused_computation.1 | loop fusion | flops 7 | bytes 17 | tf_op jit(solution)/shard_map/reduce_or | solution.py:521
  91.6 4.0 %conditional.1 = (f32[1,1,4,128,128]{4,3,2,1,0:T(8,128)}) conditional(s32[]{:T(128)} %convert_element_type.3, (s32[8,1,128]{2,1,0:T(1,128)S(1)}, f32[8,6,128,128]{3,2,1,0:T(8,128)S(1)}, f32[64,1,4,128,128]{4,3,2,1,0:T(8,128)}, f32[4,1,4,128,128]{4,3,2,1,0:T(8,128)}, f32[1,4,128,128]{3,2,1,0:T(8,128)S(1)}) %tuple.13, (s32[32,1,128]{2,1,0:T(1,128)S(1)}, ...), branch_computations={%region_1.2_spmd, %region_2.3_spmd} | conditional | bytes 6293624 | solution.py:521
  91.6 4.0 %branch_0_fun.1 = f32[1,4,128,128]{3,2,1,0:T(8,128)} custom-call(s32[8,1,128]{2,1,0:T(1,128)S(1)} %get-tuple-element.25.codes_ref, f32[8,6,128,128]{3,2,1,0:T(8,128)S(1)} %get-tuple-element.26.got_ref, f32[64,1,4,128,128]{4,3,2,1,0:T(8,128)} %get-tuple-element.27.blocks_ref, f32[4,1,4,128,128]{4,3,2,1,0:T(8,128)} %get-tuple-element.28.lefts_ref, ...), custom_call_target="tpu_custom_call" | custom-call | tf_op jit(solution)/shard_map/cond/branch_0_fun/pallas_call | solution.py:403
  (1 shorter events, 0.0 us)
Async XLA Ops:
  73.9 0.5 copy-start.3

commit v3 on v2

--- a/solution.py
+++ b/solution.py
@@ -20,7 +20,9 @@
     return lax.axis_index("row"), lax.axis_index("col"), lax.axis_index("depth")
 
 
-def meta_kernel(sizes, panels, local_ref, all_ref, send_sem, recv_sem, own_sem):
+def meta_kernel(
+    sizes, panels, local_ref, all_ref, sibling_ref, send_sem, recv_sem, own_sem, swap_sems
+):
     rows, cols, depths = sizes
     window = rows * depths
     r, c, d = position()
@@ -75,6 +77,14 @@
         )
 
     me = me_q * cols + c
+    swap = pltpu.make_async_remote_copy(
+        src_ref=local_ref,
+        dst_ref=sibling_ref,
+        send_sem=swap_sems.at[0],
+        recv_sem=swap_sems.at[1],
+        device_id=(1 - r, c, d),
+        device_id_type=MESH,
+    )
 
     @pl.loop(0, inner)
     def _(i):
@@ -84,6 +94,7 @@
     def _(off):
         copy(me, *column_mate(off)).start()
 
+    swap.start()
     own.wait()
 
     @pl.loop(1, window)
@@ -101,24 +112,32 @@
     def _(i):
         copy(me, *inner_mate(i)).wait_send()
 
+    swap.wait()
+
 
 def gather_meta(local, sizes, panels):
     devices = sizes[0] * sizes[1] * sizes[2]
     return pl.pallas_call(
         functools.partial(meta_kernel, sizes, panels),
-        out_shape=jax.ShapeDtypeStruct((devices, 1, LANES), jnp.int32),
+        out_shape=(
+            jax.ShapeDtypeStruct((devices, 1, LANES), jnp.int32),
+            jax.ShapeDtypeStruct(local.shape, jnp.int32),
+        ),
         in_specs=[pl.BlockSpec(memory_space=pltpu.VMEM)],
-        out_specs=pl.BlockSpec(memory_space=pltpu.VMEM),
+        out_specs=(pl.BlockSpec(memory_space=pltpu.VMEM),) * 2,
         scratch_shapes=[
             pltpu.SemaphoreType.DMA((devices,)),
             pltpu.SemaphoreType.DMA((devices,)),
             pltpu.SemaphoreType.DMA,
+            pltpu.SemaphoreType.DMA((2,)),
         ],
         compiler_params=pltpu.CompilerParams(collective_id=0, has_side_effects=True),
     )(local)
 
 
-def pack_kernel(sizes, dims, short, win_ref, local_ref, blocks_ref, pack_ref, codes_ref, sem):
+def pack_kernel(
+    sizes, dims, short, win_ref, local_ref, sibling_ref, blocks_ref, pack_ref, codes_ref, sem
+):
     rows, cols, depths = sizes
     local_rows, panels, slots = dims
     window = rows * depths
@@ -133,48 +152,67 @@
     def entry(q, n, row, panel, slot):
         return pltpu.make_async_copy(blocks_ref.at[row, panel, slot], pack_ref.at[q, n], sem)
 
+    pack_ref[...] = jnp.zeros_like(pack_ref)
+
     def pack_row(q, carry):
         too_long, copies = carry
         left_at = q * cols + owner
         out_at = q * cols + c
         left_count = win_ref[left_at, 0, counts_at + left_panel]
-        room = jnp.where(q == me_q, 0, limit)
-
-        def left_step(a, n):
+        on_chip = q % depths == d
+        limit_q = jnp.where(on_chip, capacity, limit)
+        room = jnp.where(q == me_q, 0, limit_q)
+        from_back = (r == 1) & jnp.logical_not(on_chip)
+
+        def left_step(a, counts):
             place = win_ref[left_at, 0, left_panel * slots + a]
             row = place % local_rows
-
-            def panel_step(panel, n):
-                out_count = win_ref[out_at, 0, counts_at + panel]
-                inner_count = local_ref[row, 0, counts_at + panel]
-
-                def inner_step(t, n):
-                    column = local_ref[row, 0, panel * slots + t]
-
-                    def out_step(s, n):
-                        hit = win_ref[out_at, 0, panel * slots + s] == column
-
-                        @pl.when(hit)
-                        def _():
-                            codes_ref[q, 0, HEAD + n] = a * counts_at + panel * slots + s
-                            codes_ref[q, 0, SOURCE + n] = (row * panels + panel) * slots + t
-
-                        @pl.when(hit & (n < room))
-                        def _():
-                            entry(q, n, row, panel, t).start()
-
-                        return n + hit.astype(jnp.int32)
-
-                    return lax.fori_loop(0, out_count, out_step, n)
-
-                return lax.fori_loop(0, inner_count, inner_step, n)
-
             mine = place // local_rows == r
-            return lax.fori_loop(0, jnp.where(mine, panels, 0), panel_step, n)
-
-        n = lax.fori_loop(0, left_count, left_step, jnp.int32(0))
+
+            def matches(inner_ref, found, n):
+                def panel_step(panel, n):
+                    out_count = win_ref[out_at, 0, counts_at + panel]
+                    inner_count = inner_ref[row, 0, counts_at + panel]
+
+                    def inner_step(t, n):
+                        column = inner_ref[row, 0, panel * slots + t]
+
+                        def out_step(s, n):
+                            hit = win_ref[out_at, 0, panel * slots + s] == column
+                            found(hit, n, panel, t, s)
+                            return n + hit.astype(jnp.int32)
+
+                        return lax.fori_loop(0, out_count, out_step, n)
+
+                    return lax.fori_loop(0, inner_count, inner_step, n)
+
+                return lax.fori_loop(0, panels, panel_step, n)
+
+            def keep(hit, n, panel, t, s):
+                @pl.when(hit)
+                def _():
+                    codes_ref[q, 0, HEAD + n] = a * counts_at + panel * slots + s
+                    codes_ref[q, 0, SOURCE + n] = (row * panels + panel) * slots + t
+
+                @pl.when(hit & (n < room))
+                def _():
+                    entry(q, jnp.where(from_back, limit - 1 - n, n), row, panel, t).start()
+
+            def skip(hit, n, panel, t, s):
+                pass
+
+            n, other = counts
+            return lax.cond(
+                mine,
+                lambda: (matches(local_ref, keep, n), other),
+                lambda: (n, matches(sibling_ref, skip, other)),
+            )
+
+        zero = jnp.int32(0)
+        n, other = lax.fori_loop(0, left_count, left_step, (zero, zero))
         codes_ref[q, 0, 0] = n
-        over = ((n > limit) & (q != me_q)).astype(jnp.int32)
+        total = jnp.where(on_chip, n, n + other)
+        over = ((total > limit_q) & (q != me_q)).astype(jnp.int32)
         return too_long | over, copies + jnp.minimum(n, room)
 
     zero = jnp.int32(0)
@@ -189,37 +227,39 @@
         entry(0, 0, 0, 0, 0).wait()
 
 
-def pack_lists(win, local, blocks, sizes, short, capacity):
+def pack_lists(win, local, sibling, blocks, sizes, short, capacity):
     local_rows, panels, slots, size, _ = blocks.shape
     window = sizes[0] * sizes[2]
+    smem = pl.BlockSpec(memory_space=pltpu.SMEM)
     return pl.pallas_call(
         functools.partial(pack_kernel, sizes, (local_rows, panels, slots), short),
         out_shape=(
             jax.ShapeDtypeStruct((window, capacity, size, size), jnp.float32),
             jax.ShapeDtypeStruct((window, 1, LANES), jnp.int32),
         ),
-        in_specs=[
-            pl.BlockSpec(memory_space=pltpu.SMEM),
-            pl.BlockSpec(memory_space=pltpu.SMEM),
-            pl.BlockSpec(memory_space=pltpu.HBM),
-        ],
-        out_specs=(pl.BlockSpec(memory_space=pltpu.VMEM), pl.BlockSpec(memory_space=pltpu.SMEM)),
+        in_specs=[smem, smem, smem, pl.BlockSpec(memory_space=pltpu.HBM)],
+        out_specs=(pl.BlockSpec(memory_space=pltpu.VMEM), smem),
         scratch_shapes=[pltpu.SemaphoreType.DMA],
         compiler_params=pltpu.CompilerParams(vmem_limit_bytes=VMEM_LIMIT),
-    )(win, local, blocks)
+    )(win, local, sibling, blocks)
 
 
 def exchange_kernel(
     sizes, panels, short, pack_ref, codes_ref, blocks_ref,
     got_ref, got_codes_ref, lefts_ref,
-    send_sem, recv_sem, left_send, left_recv, own_sem,
+    merged_ref, code_send, code_recv, left_send, left_recv,
+    swap_send, swap_recv, list_send, list_recv, own_sem,
 ):
     rows, cols, depths = sizes
     window = rows * depths
-    short_diag = pack_ref.shape[1]
+    capacity = pack_ref.shape[1]
     left_ref = blocks_ref.at[0]
     r, c, d = position()
     me = r * depths + d
+    diag = d // panels == c
+    parts = [(0, short)]
+    if capacity > short:
+        parts.append((short, capacity - short))
 
     barrier = pltpu.get_barrier_semaphore()
 
@@ -240,47 +280,79 @@
         copy.start()
     pl.semaphore_wait(barrier, window - 1 + cols - 1)
 
+    def remote(src, dst, send, recv, device):
+        return pltpu.make_async_remote_copy(
+            src_ref=src, dst_ref=dst, send_sem=send, recv_sem=recv,
+            device_id=device, device_id_type=MESH,
+        )
+
     def left_copy(slot, other):
-        return pltpu.make_async_remote_copy(
-            src_ref=left_ref,
-            dst_ref=lefts_ref.at[slot],
-            send_sem=left_send.at[other],
-            recv_sem=left_recv.at[slot],
-            device_id=(r, other, d),
-            device_id_type=MESH,
-        )
-
-    def list_copy(kind, slot, other):
-        if kind == 0:
-            src, dst = codes_ref.at[other], got_codes_ref.at[slot]
-        elif kind == 1:
-            src = pack_ref.at[other, pl.ds(0, short)]
-            dst = got_ref.at[slot, pl.ds(0, short)]
-        else:
-            src = pack_ref.at[other, pl.ds(short, short_diag - short)]
-            dst = got_ref.at[slot, pl.ds(short, short_diag - short)]
-        return pltpu.make_async_remote_copy(
-            src_ref=src,
-            dst_ref=dst,
-            send_sem=send_sem.at[kind, other],
-            recv_sem=recv_sem.at[kind, slot],
-            device_id=(other // depths, c, other % depths),
-            device_id_type=MESH,
-        )
+        return remote(
+            left_ref, lefts_ref.at[slot], left_send.at[other], left_recv.at[slot], (r, other, d)
+        )
+
+    def code_copy(slot, other):
+        return remote(
+            codes_ref.at[other], got_codes_ref.at[slot], code_send.at[other], code_recv.at[slot],
+            (other // depths, c, other % depths),
+        )
+
+    def swap_copy(part, depth):
+        first, length = parts[part]
+        there = pl.ds(first, length)
+        return remote(
+            pack_ref.at[(1 - r) * depths + depth, there], merged_ref.at[depth, there],
+            swap_send.at[part, depth], swap_recv.at[part, depth], (1 - r, c, d),
+        )
+
+    def chip_copy():
+        return remote(
+            pack_ref.at[(1 - r) * depths + d], got_ref.at[d],
+            swap_send.at[0, d], swap_recv.at[0, d], (1 - r, c, d),
+        )
+
+    def list_copy(part, slot, depth):
+        first, length = parts[part]
+        there = pl.ds(first, length)
+        return remote(
+            merged_ref.at[depth, there], got_ref.at[slot, there],
+            list_send.at[part, depth], list_recv.at[part, slot], (r, c, depth),
+        )
+
+    def each_part(wide, action):
+        action(0)
+        if len(parts) > 1:
+            @pl.when(wide)
+            def _():
+                action(1)
+
+    @pl.loop(1, depths)
+    def _(off):
+        depth = (d + off) % depths
+        each_part(diag, lambda part: swap_copy(part, depth).start())
 
     @pl.loop(1, cols)
     def _(off):
         left_copy(c, (c + off) % cols).start()
 
+    @pl.loop(1, depths)
+    def _(off):
+        depth = (d + off) % depths
+
+        def forward(part):
+            swap_copy(part, depth).wait_recv()
+            first, length = parts[part]
+            there = pl.ds(first, length)
+            merged_ref[depth, there] += pack_ref[r * depths + depth, there]
+            list_copy(part, d, depth).start()
+
+        each_part(diag, forward)
+
+    chip_copy().start()
+
     @pl.loop(1, window)
     def _(off):
-        other = (me + off) % window
-        list_copy(0, me, other).start()
-        list_copy(1, me, other).start()
-        if short_diag > short:
-            @pl.when(d // panels == c)
-            def _():
-                list_copy(2, me, other).start()
+        code_copy(me, (me + off) % window).start()
 
     for copy in own:
         copy.wait()
@@ -294,40 +366,39 @@
     @pl.loop(1, window)
     def _(off):
         other = (me + off) % window
-        list_copy(0, other, other).wait_recv()
-        list_copy(0, me, other).wait_send()
-        list_copy(1, other, other).wait_recv()
-        list_copy(1, me, other).wait_send()
-        if short_diag > short:
-            @pl.when((other % depths) // panels == c)
-            def _():
-                list_copy(2, other, other).wait_recv()
-
-            @pl.when(d // panels == c)
-            def _():
-                list_copy(2, me, other).wait_send()
+        code_copy(other, other).wait_recv()
+        code_copy(me, other).wait_send()
+
+    chip_copy().wait()
+
+    @pl.loop(1, depths)
+    def _(off):
+        depth = (d + off) % depths
+        each_part(diag, lambda part: swap_copy(part, depth).wait_send())
+        each_part(depth // panels == c, lambda part: list_copy(part, depth, depth).wait_recv())
+        each_part(diag, lambda part: list_copy(part, d, depth).wait_send())
 
 
 def exchange(pack, codes, blocks, sizes, short, ident):
-    window = pack.shape[0]
-    cols = sizes[1]
+    window, capacity, size, _ = pack.shape
+    rows, cols, depths = sizes
     panels = blocks.shape[1]
     vmem = pl.BlockSpec(memory_space=pltpu.VMEM)
+    lists = (depths, capacity, size, size)
+    sem = pltpu.SemaphoreType.DMA
     return pl.pallas_call(
         functools.partial(exchange_kernel, sizes, panels, short),
         out_shape=(
-            jax.ShapeDtypeStruct(pack.shape, jnp.float32),
+            jax.ShapeDtypeStruct(lists, jnp.float32),
             jax.ShapeDtypeStruct(codes.shape, jnp.int32),
             jax.ShapeDtypeStruct((cols,) + blocks.shape[1:], jnp.float32),
         ),
         in_specs=[vmem, vmem, pl.BlockSpec(memory_space=pltpu.HBM)],
         out_specs=(vmem,) * 3,
         scratch_shapes=[
-            pltpu.SemaphoreType.DMA((3, window)),
-            pltpu.SemaphoreType.DMA((3, window)),
-            pltpu.SemaphoreType.DMA((cols,)),
-            pltpu.SemaphoreType.DMA((cols,)),
-            pltpu.SemaphoreType.DMA((2,)),
+            pltpu.VMEM(lists, jnp.float32),
+            sem((window,)), sem((window,)), sem((cols,)), sem((cols,)),
+            sem((2, depths)), sem((2, depths)), sem((2, depths)), sem((2, depths)), sem((2,)),
         ],
         compiler_params=pltpu.CompilerParams(
             collective_id=ident, has_side_effects=True, vmem_limit_bytes=VMEM_LIMIT
@@ -337,7 +408,8 @@
 
 def multiply_into(acc_ref, lefts_ref, got_ref, blocks_ref, codes_ref, held, sems, sizes, short):
     rows, cols, depths = sizes
-    window, capacity = got_ref.shape[:2]
+    window = rows * depths
+    capacity = got_ref.shape[1]
     panels, slots = blocks_ref.shape[1:3]
     out_slots = panels * slots
     r, c, d = position()
@@ -367,12 +439,15 @@
 
     @pl.loop(0, window)
     def _(q):
-        room = jnp.where((q % depths) // panels == c, capacity, short)
-        room = jnp.where(q == me_q, 0, room)
-
-        @pl.loop(0, jnp.minimum(codes_ref[q, 0, 0], room))
+        depth = q % depths
+        on_chip = depth == d
+        room = jnp.where(on_chip | (depth // panels == c), capacity, short)
+        from_back = (q // depths == 1) & jnp.logical_not(on_chip)
+        count = jnp.where(q == me_q, 0, jnp.minimum(codes_ref[q, 0, 0], room))
+
+        @pl.loop(0, count)
         def _(n):
-            add(q, n, got_ref[q, n])
+            add(q, n, got_ref[depth, jnp.where(from_back, room - 1 - n, n)])
 
     @pl.loop(0, own)
     def _(n):
@@ -384,7 +459,7 @@
     sizes, short, codes_ref, got_ref, blocks_ref, lefts_ref, out_ref, flag_ref, held, sems
 ):
     flag_ref[0, 0] = lax.fori_loop(
-        0, got_ref.shape[0], lambda q, f: f | codes_ref[q, 0, 1], jnp.int32(0)
+        0, codes_ref.shape[0], lambda q, f: f | codes_ref[q, 0, 1], jnp.int32(0)
     )
     multiply_into(out_ref, lefts_ref, got_ref, blocks_ref, codes_ref, held, sems, sizes, short)
 
@@ -489,12 +564,12 @@
     most = slots * slots * panels
     local = jnp.concatenate([columns.reshape(local_rows, 1, panels * slots), counts[:, None, :]], 2)
     local = jnp.pad(local, ((0, 0), (0, 0), (0, LANES - local.shape[2])))
-    win = gather_meta(local, sizes, panels)
+    win, sibling = gather_meta(local, sizes, panels)
     block_shape = jax.ShapeDtypeStruct(blocks.shape[1:], jnp.float32)
     vmem = pl.BlockSpec(memory_space=pltpu.VMEM)
 
     def square_step(short, capacity, ident):
-        pack, codes = pack_lists(win, local, blocks, sizes, short, capacity)
+        pack, codes = pack_lists(win, local, sibling, blocks, sizes, short, capacity)
         got, got_codes, lefts = exchange(pack, codes, blocks, sizes, short, ident)
         square, flag = local_product(
             functools.partial(square_kernel, sizes, short),

time: 95.6 us -> 73.1 us (0.76)
  Pallas kernels: 91.4 us -> 68 us
    pallas_call x1, Pallas kernels: 53.6 us -> 30.4 us  [exchange(): pl.pallas_call(functools.partial(exchange_kernel, sizes, panels, short),...]
    pallas_call x2, Pallas kernels: 7.28 us -> 4.71 us  [local_product(): pl.pallas_call(kernel, out_shape=out_shape, in_specs=[pl.BlockSpec(memory...]
    pallas_call x1, Pallas kernels: 15.2 us -> 17.4 us  [gather_square(): pl.pallas_call(functools.partial(gather_kernel, cols), out_shape=(jax.Sha...]
    unnamed x3 -> x5, local copies, waits for them, and re-layouts: 1.28 us -> 1.97 us
where the time goes in v3:
time: 73.1 us; the launch traced here: 73 us
  Pallas kernels  68 us (93%)
  local copies, waits for them, and re-layouts  2.74 us (4%)
  other arithmetic  1.46 us (2%)
    pallas_call x1, Pallas kernels, exchange(): pl.pallas_call(functools.partial(exchange_kernel, sizes, panels, short),...  30.4 us
    pallas_call x1, Pallas kernels, gather_square(): pl.pallas_call(functools.partial(gather_kernel, cols), out_shape=(jax.Sha...  17.4 us
    pallas_call x1, Pallas kernels, gather_meta(): pl.pallas_call(functools.partial(meta_kernel, sizes, panels), out_shape=(...  9.71 us
    pallas_call x1, Pallas kernels, pack_lists(): pl.pallas_call(functools.partial(pack_kernel, sizes, (local_rows, panels,...  5.76 us
    pallas_call x2, Pallas kernels, local_product(): pl.pallas_call(kernel, out_shape=out_shape, in_specs=[pl.BlockSpec(memory...  4.71 us
    unnamed x5, local copies, waits for them, and re-layouts  1.97 us

profile of v3, /device:TPU:0, one launch (start us, length us, event | category | flops | bytes accessed | tf_op | source)
XLA Modules:
  0.0 73.0 jit_solution(2279268752336453072)
XLA Ops:
  0.0 0.8 %copy.11 = s32[64,1,4]{2,1,0:T(1,128)S(1)} copy(s32[64,1,4]{0,2,1:T(4,128)} %param.6) | data formatting | bytes 2048 | tf_op args[1]
  0.8 0.7 %copy.12 = s32[64,1,1]{2,1,0:T(1,128)S(1)} copy(s32[64,1,1]{0,2,1:T(1,128)} %bitcast.5) | data formatting | bytes 512 | tf_op jit(solution)/shard_map/broadcast_in_dim | solution.py:565
  1.5 0.1 pad_add_fusion
  1.7 9.7 %shard_map.39 = (s32[32,1,128]{2,1,0:T(1,128)S(1)}, s32[64,1,128]{2,1,0:T(1,128)S(1)}) custom-call(s32[64,1,128]{2,1,0:T(1,128)S(1)} %pad.4.local_ref), custom_call_target="tpu_custom_call" | custom-call | tf_op jit(solution)/shard_map/pallas_call | solution.py:120
  11.4 5.8 %shard_map.40 = (f32[8,6,128,128]{3,2,1,0:T(8,128)S(1)}, s32[8,1,128]{2,1,0:T(1,128)S(1)}) custom-call(s32[32,1,128]{2,1,0:T(1,128)S(1)} %get-tuple-element.55.win_ref, s32[64,1,128]{2,1,0:T(1,128)S(1)} %pad.4.local_ref, s32[64,1,128]{2,1,0:T(1,128)S(1)} %get-tuple-element.56.sibling_ref, f32[64,1,4,128,128]{4,3,2,1,0:T(8,128)} %blocks_ref.5), custom_call_target="tpu_custom_call" | custom-call | tf_op jit(solution)/shard_map/pallas_call | solution.py:234
  17.2 30.4 %shard_map.41 = (f32[4,6,128,128]{3,2,1,0:T(8,128)S(1)}, s32[8,1,128]{2,1,0:T(1,128)S(1)}, f32[4,1,4,128,128]{4,3,2,1,0:T(8,128)S(1)}) custom-call(f32[8,6,128,128]{3,2,1,0:T(8,128)S(1)} %get-tuple-element.57.pack_ref, s32[8,1,128]{2,1,0:T(1,128)S(1)} %get-tuple-element.58.codes_ref, f32[64,1,4,128,128]{4,3,2,1,0:T(8,128)} %blocks_ref.5), custom_call_target="tpu_custom_call" | custom-call | tf_op jit(solution)/shard_map/pallas_call | solution.py:389
  47.6 2.7 %shard_map.42 = (f32[1,4,128,128]{3,2,1,0:T(8,128)S(1)}, s32[1,128]{1,0:T(1,128)S(1)}) custom-call(s32[8,1,128]{2,1,0:T(1,128)S(1)} %get-tuple-element.59.codes_ref, f32[4,6,128,128]{3,2,1,0:T(8,128)S(1)} %get-tuple-element.60.got_ref, f32[64,1,4,128,128]{4,3,2,1,0:T(8,128)} %blocks_ref.5, f32[4,1,4,128,128]{4,3,2,1,0:T(8,128)S(1)} %get-tuple-element.61.lefts_ref), custom_call_target="tpu_custom_call" | custom-call | tf_op jit(solution)/shard_map/pallas_call | solution.py:478
  50.3 0.0 copy-start.5
  50.3 0.5 copy-done.5
  50.8 17.4 %shard_map.43 = (f32[4,1,4,128,128]{4,3,2,1,0:T(8,128)S(1)}, s32[4,1,128]{2,1,0:T(1,128)}) custom-call(f32[1,4,128,128]{3,2,1,0:T(8,128)S(1)} %get-tuple-element.62.square_ref, s32[1,128]{1,0:T(1,128)} %copy-done.5), custom_call_target="tpu_custom_call" | custom-call | tf_op jit(solution)/shard_map/pallas_call | solution.py:544
  68.2 1.3 %compare_reduce_fusion = pred[]{:T(512)} fusion(s32[4,1,128]{2,1,0:T(1,128)} %get-tuple-element.64), kind=kLoop, calls=%fused_computation.1 | loop fusion | flops 7 | bytes 17 | tf_op jit(solution)/shard_map/reduce_or | solution.py:596
  70.2 2.1 %conditional.1 = (f32[1,1,4,128,128]{4,3,2,1,0:T(8,128)S(1)}) conditional(s32[]{:T(128)} %convert_element_type.3, (s32[8,1,128]{2,1,0:T(1,128)S(1)}, f32[4,6,128,128]{3,2,1,0:T(8,128)S(1)}, f32[64,1,4,128,128]{4,3,2,1,0:T(8,128)}, f32[4,1,4,128,128]{4,3,2,1,0:T(8,128)S(1)}, f32[1,4,128,128]{3,2,1,0:T(8,128)S(1)}) %tuple.13, ...), branch_computations={%region_1.2_spmd, %region_2.3_spmd} | conditional | bytes 39848112 | solution.py:596
  70.2 2.1 %branch_0_fun.1 = f32[1,4,128,128]{3,2,1,0:T(8,128)S(1)} custom-call(s32[8,1,128]{2,1,0:T(1,128)S(1)} %get-tuple-element.27.codes_ref, f32[4,6,128,128]{3,2,1,0:T(8,128)S(1)} %get-tuple-element.28.got_ref, f32[64,1,4,128,128]{4,3,2,1,0:T(8,128)} %get-tuple-element.29.blocks_ref, f32[4,1,4,128,128]{4,3,2,1,0:T(8,128)S(1)} %get-tuple-element.30.lefts_ref, ...), custom_call_target="tpu_custom_call" | custom-call | tf_op jit(solution)/shard_map/cond/branch_0_fun/pallas_call | solution.py:478
  72.3 0.0 copy-start.7
  72.3 0.7 copy-done.7
  (1 shorter events, 0.0 us)
Async XLA Ops:
  50.3 0.5 copy-start.5
  72.3 0.7 copy-start.7

commit v4 on v3

--- a/solution.py
+++ b/solution.py
@@ -248,7 +248,7 @@
     sizes, panels, short, pack_ref, codes_ref, blocks_ref,
     got_ref, got_codes_ref, lefts_ref,
     merged_ref, code_send, code_recv, left_send, left_recv,
-    swap_send, swap_recv, list_send, list_recv, own_sem,
+    swap_send, swap_recv, list_send, list_recv, relay_ref, relay_send, relay_recv, own_sem,
 ):
     rows, cols, depths = sizes
     window = rows * depths
@@ -257,9 +257,15 @@
     r, c, d = position()
     me = r * depths + d
     diag = d // panels == c
-    parts = [(0, short)]
-    if capacity > short:
-        parts.append((short, capacity - short))
+    parts = [(0, short, 0)]
+    extra = capacity - short
+    ways = [1, 2] if cols == 4 and extra >= 4 else []
+    straight = extra // 4 if ways else extra
+    if extra:
+        parts.append((short, straight, 0))
+    if ways:
+        parts.append((short + straight, straight, 1))
+        parts.append((short + 2 * straight, extra - 2 * straight, 2))
 
     barrier = pltpu.get_barrier_semaphore()
 
@@ -271,6 +277,12 @@
     @pl.loop(1, cols)
     def _(off):
         pl.semaphore_signal(barrier, inc=1, device_id=(r, (c + off) % cols, d), device_id_type=MESH)
+
+    for way in ways:
+        @pl.loop(1, depths)
+        def _(off):
+            device = (r, c ^ way, (d + off) % depths)
+            pl.semaphore_signal(barrier, inc=1, device_id=device, device_id_type=MESH)
 
     own = [
         pltpu.make_async_copy(codes_ref.at[me], got_codes_ref.at[me], own_sem.at[0]),
@@ -278,7 +290,7 @@
     ]
     for copy in own:
         copy.start()
-    pl.semaphore_wait(barrier, window - 1 + cols - 1)
+    pl.semaphore_wait(barrier, window - 1 + cols - 1 + len(ways) * (depths - 1))
 
     def remote(src, dst, send, recv, device):
         return pltpu.make_async_remote_copy(
@@ -298,7 +310,7 @@
         )
 
     def swap_copy(part, depth):
-        first, length = parts[part]
+        first, length, way = parts[part]
         there = pl.ds(first, length)
         return remote(
             pack_ref.at[(1 - r) * depths + depth, there], merged_ref.at[depth, there],
@@ -312,11 +324,20 @@
         )
 
     def list_copy(part, slot, depth):
-        first, length = parts[part]
+        first, length, way = parts[part]
         there = pl.ds(first, length)
+        target = relay_ref.at[way - 1, slot % panels, pl.ds(0, length)] if way else got_ref.at[slot, there]
         return remote(
-            merged_ref.at[depth, there], got_ref.at[slot, there],
-            list_send.at[part, depth], list_recv.at[part, slot], (r, c, depth),
+            merged_ref.at[depth, there], target,
+            list_send.at[part, depth], list_recv.at[part, slot], (r, c ^ way, depth),
+        )
+
+    def relay_copy(part, depth):
+        first, length, way = parts[part]
+        return remote(
+            relay_ref.at[way - 1, depth % panels, pl.ds(0, length)],
+            got_ref.at[depth, pl.ds(first, length)],
+            relay_send.at[part, depth], relay_recv.at[part, depth], (r, c ^ way, d),
         )
 
     def each_part(wide, action):
@@ -324,7 +345,21 @@
         if len(parts) > 1:
             @pl.when(wide)
             def _():
-                action(1)
+                for part in range(1, len(parts)):
+                    action(part)
+
+    def arrival(part, depth):
+        return list_copy(part, depth, depth)
+
+    def each_relay(action):
+        for part, (first, length, way) in enumerate(parts):
+            if way:
+                for i in range(panels):
+                    depth = (c ^ way) * panels + i
+
+                    @pl.when(depth != d)
+                    def _():
+                        action(part, depth)
 
     @pl.loop(1, depths)
     def _(off):
@@ -341,7 +376,7 @@
 
         def forward(part):
             swap_copy(part, depth).wait_recv()
-            first, length = parts[part]
+            first, length, way = parts[part]
             there = pl.ds(first, length)
             merged_ref[depth, there] += pack_ref[r * depths + depth, there]
             list_copy(part, d, depth).start()
@@ -354,6 +389,12 @@
     def _(off):
         code_copy(me, (me + off) % window).start()
 
+    def pass_on(part, depth):
+        list_copy(part, depth, d).wait_recv()
+        relay_copy(part, depth).start()
+
+    each_relay(pass_on)
+
     for copy in own:
         copy.wait()
 
@@ -375,8 +416,13 @@
     def _(off):
         depth = (d + off) % depths
         each_part(diag, lambda part: swap_copy(part, depth).wait_send())
-        each_part(depth // panels == c, lambda part: list_copy(part, depth, depth).wait_recv())
+        each_part(
+            depth // panels == c,
+            lambda part: (relay_copy if parts[part][2] else arrival)(part, depth).wait_recv(),
+        )
         each_part(diag, lambda part: list_copy(part, d, depth).wait_send())
+
+    each_relay(lambda part, depth: relay_copy(part, depth).wait_send())
 
 
 def exchange(pack, codes, blocks, sizes, short, ident):
@@ -398,7 +444,9 @@
         scratch_shapes=[
             pltpu.VMEM(lists, jnp.float32),
             sem((window,)), sem((window,)), sem((cols,)), sem((cols,)),
-            sem((2, depths)), sem((2, depths)), sem((2, depths)), sem((2, depths)), sem((2,)),
+            sem((4, depths)), sem((4, depths)), sem((4, depths)), sem((4, depths)),
+            pltpu.VMEM((2, panels, capacity, size, size), jnp.float32),
+            sem((4, depths)), sem((4, depths)), sem((2,)),
         ],
         compiler_params=pltpu.CompilerParams(
             collective_id=ident, has_side_effects=True, vmem_limit_bytes=VMEM_LIMIT
@@ -458,9 +506,8 @@
 def square_kernel(
     sizes, short, codes_ref, got_ref, blocks_ref, lefts_ref, out_ref, flag_ref, held, sems
 ):
-    flag_ref[0, 0] = lax.fori_loop(
-        0, codes_ref.shape[0], lambda q, f: f | codes_ref[q, 0, 1], jnp.int32(0)
-    )
+    flag = lax.fori_loop(0, codes_ref.shape[0], lambda q, f: f | codes_ref[q, 0, 1], jnp.int32(0))
+    flag_ref[...] = jnp.full(flag_ref.shape, flag, jnp.int32)
     multiply_into(out_ref, lefts_ref, got_ref, blocks_ref, codes_ref, held, sems, sizes, short)
 
 
@@ -493,7 +540,9 @@
     )(codes, got, blocks, lefts, *extra)
 
 
-def gather_kernel(cols, square_ref, flag_ref, squares_ref, flags_ref, send_sem, recv_sem, own_sem):
+def gather_kernel(
+    cols, square_ref, flag_ref, squares_ref, any_ref, flags_ref, send_sem, recv_sem, own_sem
+):
     r, c, d = position()
     barrier = pltpu.get_barrier_semaphore()
 
@@ -538,6 +587,8 @@
         for copy in copies(c, other):
             copy.wait_send()
 
+    any_ref[...] = jnp.max(flags_ref[...], axis=0)
+
 
 def gather_square(square, flag, cols, ident):
     vmem = pl.BlockSpec(memory_space=pltpu.VMEM)
@@ -545,11 +596,12 @@
         functools.partial(gather_kernel, cols),
         out_shape=(
             jax.ShapeDtypeStruct((cols,) + square.shape, jnp.float32),
-            jax.ShapeDtypeStruct((cols,) + flag.shape, jnp.int32),
+            jax.ShapeDtypeStruct(flag.shape, jnp.int32),
         ),
         in_specs=[vmem] * 2,
         out_specs=(vmem,) * 2,
         scratch_shapes=[
+            pltpu.VMEM((cols,) + flag.shape, jnp.int32),
             pltpu.SemaphoreType.DMA((2, cols)),
             pltpu.SemaphoreType.DMA((2, cols)),
             pltpu.SemaphoreType.DMA((2,)),
@@ -575,10 +627,10 @@
             functools.partial(square_kernel, sizes, short),
             got_codes, got, blocks, lefts, (),
             (block_shape, jax.ShapeDtypeStruct((1, LANES), jnp.int32)),
-            (vmem, pl.BlockSpec(memory_space=pltpu.SMEM)),
-        )
-        squares, flags = gather_square(square, flag, cols, ident + 1)
-        return got, got_codes, square, squares, flags
+            (vmem, vmem),
+        )
+        squares, too_long = gather_square(square, flag, cols, ident + 1)
+        return got, got_codes, square, squares, too_long
 
     def cube_step(short, got, got_codes, square, squares):
         return local_product(
@@ -587,13 +639,13 @@
         )
 
     short = min(SHORT, most)
-    *lists, flags = square_step(short, min(SHORT_DIAG, most), 1)
+    *lists, too_long = square_step(short, min(SHORT_DIAG, most), 1)
 
     def again():
         *lists, _ = square_step(most, most, 3)
         return cube_step(most, *lists)
 
-    out = lax.cond(jnp.any(flags[:, 0, 0] != 0), again, lambda: cube_step(short, *lists))
+    out = lax.cond(too_long[0, 0] != 0, again, lambda: cube_step(short, *lists))
     return out[None]
 
 

time: 73.1 us -> 74.3 us (1.016)
  the two profiles are of different devices: /device:TPU:0 before, /device:TPU:18 now
where the time goes in v4:
time: 74.3 us; the launch traced here: 74.8 us
  Pallas kernels  71.1 us (96%)
  local copies, waits for them, and re-layouts  2.74 us (4%)
  between operations  0.77 us (1%)
    pallas_call x1, Pallas kernels, exchange(): pl.pallas_call(functools.partial(exchange_kernel, sizes, panels, short),...  36 us
    pallas_call x1, Pallas kernels, gather_square(): pl.pallas_call(functools.partial(gather_kernel, cols), out_shape=(jax.Sha...  16.6 us
    pallas_call x1, Pallas kernels, gather_meta(): pl.pallas_call(functools.partial(meta_kernel, sizes, panels), out_shape=(...  7.23 us
    pallas_call x2, Pallas kernels, local_product(): pl.pallas_call(kernel, out_shape=out_shape, in_specs=[pl.BlockSpec(memory...  5.79 us
    pallas_call x1, Pallas kernels, pack_lists(): pl.pallas_call(functools.partial(pack_kernel, sizes, (local_rows, panels,...  5.57 us
    unnamed x5, local copies, waits for them, and re-layouts  1.97 us

profile of v4, /device:TPU:18, one launch (start us, length us, event | category | flops | bytes accessed | tf_op | source)
XLA Modules:
  0.0 74.8 jit_solution(7629572184716330940)
XLA Ops:
  0.0 0.8 %copy.11 = s32[64,1,4]{2,1,0:T(1,128)S(1)} copy(s32[64,1,4]{0,2,1:T(4,128)} %param.6) | data formatting | bytes 2048 | tf_op args[1]
  0.8 0.7 copy.12
  1.5 0.1 pad_add_fusion
  1.7 7.2 %shard_map.39 = (s32[32,1,128]{2,1,0:T(1,128)S(1)}, s32[64,1,128]{2,1,0:T(1,128)S(1)}) custom-call(s32[64,1,128]{2,1,0:T(1,128)S(1)} %pad.4.local_ref), custom_call_target="tpu_custom_call" | custom-call | tf_op jit(solution)/shard_map/pallas_call | solution.py:120
  8.9 5.6 %shard_map.40 = (f32[8,6,128,128]{3,2,1,0:T(8,128)S(1)}, s32[8,1,128]{2,1,0:T(1,128)S(1)}) custom-call(s32[32,1,128]{2,1,0:T(1,128)S(1)} %get-tuple-element.55.win_ref, s32[64,1,128]{2,1,0:T(1,128)S(1)} %pad.4.local_ref, s32[64,1,128]{2,1,0:T(1,128)S(1)} %get-tuple-element.56.sibling_ref, f32[64,1,4,128,128]{4,3,2,1,0:T(8,128)} %blocks_ref.5), custom_call_target="tpu_custom_call" | custom-call | tf_op jit(solution)/shard_map/pallas_call | solution.py:234
  14.5 36.0 %shard_map.41 = (f32[4,6,128,128]{3,2,1,0:T(8,128)S(1)}, s32[8,1,128]{2,1,0:T(1,128)S(1)}, f32[4,1,4,128,128]{4,3,2,1,0:T(8,128)S(1)}) custom-call(f32[8,6,128,128]{3,2,1,0:T(8,128)S(1)} %get-tuple-element.57.pack_ref, s32[8,1,128]{2,1,0:T(1,128)S(1)} %get-tuple-element.58.codes_ref, f32[64,1,4,128,128]{4,3,2,1,0:T(8,128)} %blocks_ref.5), custom_call_target="tpu_custom_call" | custom-call | tf_op jit(solution)/shard_map/pallas_call | solution.py:435
  50.5 2.9 %shard_map.42 = (f32[1,4,128,128]{3,2,1,0:T(8,128)S(1)}, s32[1,128]{1,0:T(1,128)S(1)}) custom-call(s32[8,1,128]{2,1,0:T(1,128)S(1)} %get-tuple-element.59.codes_ref, f32[4,6,128,128]{3,2,1,0:T(8,128)S(1)} %get-tuple-element.60.got_ref, f32[64,1,4,128,128]{4,3,2,1,0:T(8,128)} %blocks_ref.5, f32[4,1,4,128,128]{4,3,2,1,0:T(8,128)S(1)} %get-tuple-element.61.lefts_ref), custom_call_target="tpu_custom_call" | custom-call | tf_op jit(solution)/shard_map/pallas_call | solution.py:525
  53.4 0.0 copy-start.5
  53.4 0.5 copy-done.5
  53.9 16.6 %shard_map.43 = (f32[4,1,4,128,128]{4,3,2,1,0:T(8,128)S(1)}, s32[1,128]{1,0:T(1,128)}) custom-call(f32[1,4,128,128]{3,2,1,0:T(8,128)S(1)} %get-tuple-element.62.square_ref, s32[1,128]{1,0:T(1,128)} %copy-done.5), custom_call_target="tpu_custom_call" | custom-call | tf_op jit(solution)/shard_map/pallas_call | solution.py:595
  71.1 2.9 %conditional.1 = (f32[1,1,4,128,128]{4,3,2,1,0:T(8,128)S(1)}) conditional(s32[]{:T(128)} %bitcast.3, (s32[8,1,128]{2,1,0:T(1,128)S(1)}, f32[4,6,128,128]{3,2,1,0:T(8,128)S(1)}, f32[64,1,4,128,128]{4,3,2,1,0:T(8,128)}, f32[4,1,4,128,128]{4,3,2,1,0:T(8,128)S(1)}, f32[1,4,128,128]{3,2,1,0:T(8,128)S(1)}) %tuple.13, (s32[32,1,128]{2,1,0:T(1,128)S(1)}, ...), branch_computations={%region_0.1_spmd, %region_1.2_spmd} | conditional | bytes 39848112 | solution.py:648
  71.1 2.9 %branch_0_fun.1 = f32[1,4,128,128]{3,2,1,0:T(8,128)S(1)} custom-call(s32[8,1,128]{2,1,0:T(1,128)S(1)} %get-tuple-element.27.codes_ref, f32[4,6,128,128]{3,2,1,0:T(8,128)S(1)} %get-tuple-element.28.got_ref, f32[64,1,4,128,128]{4,3,2,1,0:T(8,128)} %get-tuple-element.29.blocks_ref, f32[4,1,4,128,128]{4,3,2,1,0:T(8,128)S(1)} %get-tuple-element.30.lefts_ref, ...), custom_call_target="tpu_custom_call" | custom-call | tf_op jit(solution)/shard_map/cond/branch_0_fun/pallas_call | solution.py:525
  74.0 0.0 copy-start.7
  74.1 0.7 copy-done.7
  (1 shorter events, 0.0 us)
Async XLA Ops:
  53.4 0.5 copy-start.5
  74.0 0.7 copy-start.7

commit v5 on v3

--- a/solution.py
+++ b/solution.py
@@ -18,6 +18,72 @@
 
 def position():
     return lax.axis_index("row"), lax.axis_index("col"), lax.axis_index("depth")
+
+
+def spread(cols, slots, src_ref, dst_ref, send, recv):
+    r, c, d = position()
+
+    def remote(src, dst, send, recv, column):
+        return pltpu.make_async_remote_copy(
+            src_ref=src, dst_ref=dst, send_sem=send, recv_sem=recv,
+            device_id=(r, column, d), device_id_type=MESH,
+        )
+
+    if cols != 4 or slots % 2:
+        def copy(slot, other):
+            return remote(src_ref, dst_ref.at[slot], send.at[0, other], recv.at[0, slot], other)
+
+        def begin():
+            @pl.loop(1, cols)
+            def _(off):
+                copy(c, (c + off) % cols).start()
+
+        def end():
+            @pl.loop(1, cols)
+            def _(off):
+                other = (c + off) % cols
+                copy(other, other).wait_recv()
+                copy(c, other).wait_send()
+
+        return begin, lambda: None, end
+
+    def half(ref, h):
+        return ref.at[:, pl.ds(h * (slots // 2), slots // 2)]
+
+    def direct(h, way):
+        return remote(
+            half(src_ref, h), half(dst_ref.at[c], h), send.at[h, way - 1], recv.at[h, c], c ^ way
+        )
+
+    def arrival(h, way):
+        there = half(dst_ref.at[c ^ way], h)
+        return remote(half(src_ref, h), there, send.at[h, 0], recv.at[h, c ^ way], c ^ 1)
+
+    def onward(h):
+        origin = c ^ (1 + h)
+        there = half(dst_ref.at[origin], h)
+        return remote(there, there, send.at[h, 2], recv.at[h, origin], c ^ (2 - h))
+
+    sent = [(0, 1), (1, 2), (1, 1), (0, 2)]
+
+    def begin():
+        for h, way in sent:
+            direct(h, way).start()
+
+    def pass_on():
+        for h in (0, 1):
+            arrival(h, 1 + h).wait_recv()
+            onward(h).start()
+
+    def end():
+        for h, way in ((1, 1), (0, 2), (0, 3), (1, 3)):
+            arrival(h, way).wait_recv()
+        for h, way in sent:
+            direct(h, way).wait_send()
+        for h in (0, 1):
+            onward(h).wait_send()
+
+    return begin, pass_on, end
 
 
 def meta_kernel(
@@ -152,8 +218,6 @@
     def entry(q, n, row, panel, slot):
         return pltpu.make_async_copy(blocks_ref.at[row, panel, slot], pack_ref.at[q, n], sem)
 
-    pack_ref[...] = jnp.zeros_like(pack_ref)
-
     def pack_row(q, carry):
         too_long, copies = carry
         left_at = q * cols + owner
@@ -286,10 +350,9 @@
             device_id=device, device_id_type=MESH,
         )
 
-    def left_copy(slot, other):
-        return remote(
-            left_ref, lefts_ref.at[slot], left_send.at[other], left_recv.at[slot], (r, other, d)
-        )
+    begin, pass_on, end = spread(
+        cols, blocks_ref.shape[2], left_ref, lefts_ref, left_send, left_recv
+    )
 
     def code_copy(slot, other):
         return remote(
@@ -331,9 +394,7 @@
         depth = (d + off) % depths
         each_part(diag, lambda part: swap_copy(part, depth).start())
 
-    @pl.loop(1, cols)
-    def _(off):
-        left_copy(c, (c + off) % cols).start()
+    begin()
 
     @pl.loop(1, depths)
     def _(off):
@@ -342,8 +403,13 @@
         def forward(part):
             swap_copy(part, depth).wait_recv()
             first, length = parts[part]
-            there = pl.ds(first, length)
-            merged_ref[depth, there] += pack_ref[r * depths + depth, there]
+            q = r * depths + depth
+            count = jnp.broadcast_to(codes_ref[q, 0:1, 0:1], pack_ref.shape[2:])
+            for place in range(first, first + length):
+                rank = jnp.where(r == 1, jnp.where(diag, capacity, short) - 1 - place, place)
+                merged_ref[depth, place] = jnp.where(
+                    rank < count, pack_ref[q, place], merged_ref[depth, place]
+                )
             list_copy(part, d, depth).start()
 
         each_part(diag, forward)
@@ -357,11 +423,8 @@
     for copy in own:
         copy.wait()
 
-    @pl.loop(1, cols)
-    def _(off):
-        other = (c + off) % cols
-        left_copy(other, other).wait_recv()
-        left_copy(c, other).wait_send()
+    pass_on()
+    end()
 
     @pl.loop(1, window)
     def _(off):
@@ -397,7 +460,7 @@
         out_specs=(vmem,) * 3,
         scratch_shapes=[
             pltpu.VMEM(lists, jnp.float32),
-            sem((window,)), sem((window,)), sem((cols,)), sem((cols,)),
+            sem((window,)), sem((window,)), sem((2, max(3, cols))), sem((2, cols)),
             sem((2, depths)), sem((2, depths)), sem((2, depths)), sem((2, depths)), sem((2,)),
         ],
         compiler_params=pltpu.CompilerParams(
@@ -458,9 +521,8 @@
 def square_kernel(
     sizes, short, codes_ref, got_ref, blocks_ref, lefts_ref, out_ref, flag_ref, held, sems
 ):
-    flag_ref[0, 0] = lax.fori_loop(
-        0, codes_ref.shape[0], lambda q, f: f | codes_ref[q, 0, 1], jnp.int32(0)
-    )
+    flag = lax.fori_loop(0, codes_ref.shape[0], lambda q, f: f | codes_ref[q, 0, 1], jnp.int32(0))
+    flag_ref[...] = jnp.full(flag_ref.shape, flag, jnp.int32)
     multiply_into(out_ref, lefts_ref, got_ref, blocks_ref, codes_ref, held, sems, sizes, short)
 
 
@@ -493,7 +555,10 @@
     )(codes, got, blocks, lefts, *extra)
 
 
-def gather_kernel(cols, square_ref, flag_ref, squares_ref, flags_ref, send_sem, recv_sem, own_sem):
+def gather_kernel(
+    cols, square_ref, flag_ref, squares_ref, any_ref, flags_ref,
+    send_sem, recv_sem, flag_send, flag_recv, own_sem,
+):
     r, c, d = position()
     barrier = pltpu.get_barrier_semaphore()
 
@@ -501,42 +566,45 @@
     def _(off):
         pl.semaphore_signal(barrier, inc=1, device_id=(r, (c + off) % cols, d), device_id_type=MESH)
 
-    pairs = ((square_ref, squares_ref), (flag_ref, flags_ref))
     own = [
-        pltpu.make_async_copy(src, dst.at[c], own_sem.at[i]) for i, (src, dst) in enumerate(pairs)
+        pltpu.make_async_copy(square_ref, squares_ref.at[c], own_sem.at[0]),
+        pltpu.make_async_copy(flag_ref, flags_ref.at[c], own_sem.at[1]),
     ]
     for copy in own:
         copy.start()
+    begin, pass_on, end = spread(
+        cols, square_ref.shape[1], square_ref, squares_ref, send_sem, recv_sem
+    )
     pl.semaphore_wait(barrier, cols - 1)
 
-    def copies(slot, other):
-        return [
-            pltpu.make_async_remote_copy(
-                src_ref=src,
-                dst_ref=dst.at[slot],
-                send_sem=send_sem.at[i, other],
-                recv_sem=recv_sem.at[i, slot],
-                device_id=(r, other, d),
-                device_id_type=MESH,
-            )
-            for i, (src, dst) in enumerate(pairs)
-        ]
+    def flag_copy(slot, other):
+        return pltpu.make_async_remote_copy(
+            src_ref=flag_ref,
+            dst_ref=flags_ref.at[slot],
+            send_sem=flag_send.at[other],
+            recv_sem=flag_recv.at[slot],
+            device_id=(r, other, d),
+            device_id_type=MESH,
+        )
+
+    begin()
 
     @pl.loop(1, cols)
     def _(off):
-        for copy in copies(c, (c + off) % cols):
-            copy.start()
-
+        flag_copy(c, (c + off) % cols).start()
+
+    pass_on()
     for copy in own:
         copy.wait()
 
     @pl.loop(1, cols)
     def _(off):
         other = (c + off) % cols
-        for copy in copies(other, other):
-            copy.wait_recv()
-        for copy in copies(c, other):
-            copy.wait_send()
+        flag_copy(other, other).wait_recv()
+        flag_copy(c, other).wait_send()
+
+    end()
+    any_ref[...] = jnp.max(flags_ref[...], axis=0)
 
 
 def gather_square(square, flag, cols, ident):
@@ -545,13 +613,16 @@
         functools.partial(gather_kernel, cols),
         out_shape=(
             jax.ShapeDtypeStruct((cols,) + square.shape, jnp.float32),
-            jax.ShapeDtypeStruct((cols,) + flag.shape, jnp.int32),
+            jax.ShapeDtypeStruct(flag.shape, jnp.int32),
         ),
         in_specs=[vmem] * 2,
         out_specs=(vmem,) * 2,
         scratch_shapes=[
+            pltpu.VMEM((cols,) + flag.shape, jnp.int32),
+            pltpu.SemaphoreType.DMA((2, max(3, cols))),
             pltpu.SemaphoreType.DMA((2, cols)),
-            pltpu.SemaphoreType.DMA((2, cols)),
+            pltpu.SemaphoreType.DMA((cols,)),
+            pltpu.SemaphoreType.DMA((cols,)),
             pltpu.SemaphoreType.DMA((2,)),
         ],
         compiler_params=pltpu.CompilerParams(collective_id=ident, has_side_effects=True),
@@ -575,10 +646,10 @@
             functools.partial(square_kernel, sizes, short),
             got_codes, got, blocks, lefts, (),
             (block_shape, jax.ShapeDtypeStruct((1, LANES), jnp.int32)),
-            (vmem, pl.BlockSpec(memory_space=pltpu.SMEM)),
-        )
-        squares, flags = gather_square(square, flag, cols, ident + 1)
-        return got, got_codes, square, squares, flags
+            (vmem, vmem),
+        )
+        squares, too_long = gather_square(square, flag, cols, ident + 1)
+        return got, got_codes, square, squares, too_long
 
     def cube_step(short, got, got_codes, square, squares):
         return local_product(
@@ -587,13 +658,13 @@
         )
 
     short = min(SHORT, most)
-    *lists, flags = square_step(short, min(SHORT_DIAG, most), 1)
+    *lists, too_long = square_step(short, min(SHORT_DIAG, most), 1)
 
     def again():
         *lists, _ = square_step(most, most, 3)
         return cube_step(most, *lists)
 
-    out = lax.cond(jnp.any(flags[:, 0, 0] != 0), again, lambda: cube_step(short, *lists))
+    out = lax.cond(too_long[0, 0] != 0, again, lambda: cube_step(short, *lists))
     return out[None]
 
 

time: 73.1 us -> 68.9 us (0.943)
  Pallas kernels: 68 us -> 64.9 us
  other arithmetic: 1.46 us -> 0.13 us
    pallas_call x1, Pallas kernels: 17.4 us -> 14.8 us  [gather_square(): pl.pallas_call(functools.partial(gather_kernel, cols), out_shape=(jax.Sha...]
    reduce_or x1 -> x0, other arithmetic: 1.33 us -> none  [body(): jnp.any(flags[:, 0, 0] != 0)]
where the time goes in v5:
time: 68.9 us; the launch traced here: 68.5 us
  Pallas kernels  64.9 us (94%)
  local copies, waits for them, and re-layouts  2.74 us (4%)
  between operations  0.77 us (1%)
    pallas_call x1, Pallas kernels, exchange(): pl.pallas_call(functools.partial(exchange_kernel, sizes, panels, short),...  30.4 us
    pallas_call x1, Pallas kernels, gather_square(): pl.pallas_call(functools.partial(gather_kernel, cols), out_shape=(jax.Sha...  14.8 us
    pallas_call x1, Pallas kernels, gather_meta(): pl.pallas_call(functools.partial(meta_kernel, sizes, panels), out_shape=(...  9.71 us
    pallas_call x1, Pallas kernels, pack_lists(): pl.pallas_call(functools.partial(pack_kernel, sizes, (local_rows, panels,...  5.93 us
    pallas_call x2, Pallas kernels, local_product(): pl.pallas_call(kernel, out_shape=out_shape, in_specs=[pl.BlockSpec(memory...  4.12 us
    unnamed x5, local copies, waits for them, and re-layouts  1.97 us

profile of v5, /device:TPU:0, one launch (start us, length us, event | category | flops | bytes accessed | tf_op | source)
XLA Modules:
  0.0 68.5 jit_solution(585186141279403384)
XLA Ops:
  0.0 0.8 %copy.11 = s32[64,1,4]{2,1,0:T(1,128)S(1)} copy(s32[64,1,4]{0,2,1:T(4,128)} %param.6) | data formatting | bytes 2048 | tf_op args[1]
  0.8 0.7 %copy.12 = s32[64,1,1]{2,1,0:T(1,128)S(1)} copy(s32[64,1,1]{0,2,1:T(1,128)} %bitcast.7) | data formatting | bytes 512 | tf_op jit(solution)/shard_map/broadcast_in_dim | solution.py:636
  1.5 0.1 pad_add_fusion
  1.7 9.7 %shard_map.39 = (s32[32,1,128]{2,1,0:T(1,128)S(1)}, s32[64,1,128]{2,1,0:T(1,128)S(1)}) custom-call(s32[64,1,128]{2,1,0:T(1,128)S(1)} %pad.4.local_ref), custom_call_target="tpu_custom_call" | custom-call | tf_op jit(solution)/shard_map/pallas_call | solution.py:186
  11.4 5.9 %shard_map.40 = (f32[8,6,128,128]{3,2,1,0:T(8,128)S(1)}, s32[8,1,128]{2,1,0:T(1,128)S(1)}) custom-call(s32[32,1,128]{2,1,0:T(1,128)S(1)} %get-tuple-element.55.win_ref, s32[64,1,128]{2,1,0:T(1,128)S(1)} %pad.4.local_ref, s32[64,1,128]{2,1,0:T(1,128)S(1)} %get-tuple-element.56.sibling_ref, f32[64,1,4,128,128]{4,3,2,1,0:T(8,128)} %blocks_ref.5), custom_call_target="tpu_custom_call" | custom-call | tf_op jit(solution)/shard_map/pallas_call | solution.py:298
  17.3 30.4 %shard_map.41 = (f32[4,6,128,128]{3,2,1,0:T(8,128)S(1)}, s32[8,1,128]{2,1,0:T(1,128)S(1)}, f32[4,1,4,128,128]{4,3,2,1,0:T(8,128)S(1)}) custom-call(f32[8,6,128,128]{3,2,1,0:T(8,128)S(1)} %get-tuple-element.57.pack_ref, s32[8,1,128]{2,1,0:T(1,128)S(1)} %get-tuple-element.58.codes_ref, f32[64,1,4,128,128]{4,3,2,1,0:T(8,128)} %blocks_ref.5), custom_call_target="tpu_custom_call" | custom-call | tf_op jit(solution)/shard_map/pallas_call | solution.py:452
  47.7 2.1 %shard_map.42 = (f32[1,4,128,128]{3,2,1,0:T(8,128)S(1)}, s32[1,128]{1,0:T(1,128)S(1)}) custom-call(s32[8,1,128]{2,1,0:T(1,128)S(1)} %get-tuple-element.59.codes_ref, f32[4,6,128,128]{3,2,1,0:T(8,128)S(1)} %get-tuple-element.60.got_ref, f32[64,1,4,128,128]{4,3,2,1,0:T(8,128)} %blocks_ref.5, f32[4,1,4,128,128]{4,3,2,1,0:T(8,128)S(1)} %get-tuple-element.61.lefts_ref), custom_call_target="tpu_custom_call" | custom-call | tf_op jit(solution)/shard_map/pallas_call | solution.py:540
  49.8 0.0 copy-start.5
  49.8 0.5 copy-done.5
  50.3 14.8 %shard_map.43 = (f32[4,1,4,128,128]{4,3,2,1,0:T(8,128)S(1)}, s32[1,128]{1,0:T(1,128)}) custom-call(f32[1,4,128,128]{3,2,1,0:T(8,128)S(1)} %get-tuple-element.62.square_ref, s32[1,128]{1,0:T(1,128)} %copy-done.5), custom_call_target="tpu_custom_call" | custom-call | tf_op jit(solution)/shard_map/pallas_call | solution.py:612
  65.8 2.1 %conditional.1 = (f32[1,1,4,128,128]{4,3,2,1,0:T(8,128)S(1)}) conditional(s32[]{:T(128)} %bitcast.3, (s32[8,1,128]{2,1,0:T(1,128)S(1)}, f32[4,6,128,128]{3,2,1,0:T(8,128)S(1)}, f32[64,1,4,128,128]{4,3,2,1,0:T(8,128)}, f32[4,1,4,128,128]{4,3,2,1,0:T(8,128)S(1)}, f32[1,4,128,128]{3,2,1,0:T(8,128)S(1)}) %tuple.13, (s32[32,1,128]{2,1,0:T(1,128)S(1)}, ...), branch_computations={%region_0.1_spmd, %region_1.2_spmd} | conditional | bytes 39848112 | solution.py:667
  65.8 2.1 %branch_0_fun.1 = f32[1,4,128,128]{3,2,1,0:T(8,128)S(1)} custom-call(s32[8,1,128]{2,1,0:T(1,128)S(1)} %get-tuple-element.27.codes_ref, f32[4,6,128,128]{3,2,1,0:T(8,128)S(1)} %get-tuple-element.28.got_ref, f32[64,1,4,128,128]{4,3,2,1,0:T(8,128)} %get-tuple-element.29.blocks_ref, f32[4,1,4,128,128]{4,3,2,1,0:T(8,128)S(1)} %get-tuple-element.30.lefts_ref, ...), custom_call_target="tpu_custom_call" | custom-call | tf_op jit(solution)/shard_map/cond/branch_0_fun/pallas_call | solution.py:540
  67.8 0.0 copy-start.7
  67.8 0.7 %copy-done.7 = f32[1,1,4,128,128]{4,3,2,1,0:T(8,128)} copy-done((f32[1,1,4,128,128]{4,3,2,1,0:T(8,128)}, f32[1,1,4,128,128]{4,3,2,1,0:T(8,128)S(1)}, u32[]{:S(2)}) %copy-start.7) | copy-done | bytes 262168
  (1 shorter events, 0.0 us)
Async XLA Ops:
  49.8 0.5 copy-start.5
  67.8 0.7 %copy-start.7 = (f32[1,1,4,128,128]{4,3,2,1,0:T(8,128)}, f32[1,1,4,128,128]{4,3,2,1,0:T(8,128)S(1)}, u32[]{:S(2)}) copy-start(f32[1,1,4,128,128]{4,3,2,1,0:T(8,128)S(1)} %get-tuple-element.69) | copy-start | bytes 786436

commit v6 on v5

--- a/solution.py
+++ b/solution.py
@@ -10,8 +10,7 @@
 MESH = pl.DeviceIdType.MESH
 LANES = 128
 VMEM_LIMIT = 48 << 20
-SHORT = 2
-SHORT_DIAG = 6
+TIERS = ((2, 6), (4, 8))
 HEAD = 2
 SOURCE = LANES // 2
 
@@ -312,7 +311,7 @@
     sizes, panels, short, pack_ref, codes_ref, blocks_ref,
     got_ref, got_codes_ref, lefts_ref,
     merged_ref, code_send, code_recv, left_send, left_recv,
-    swap_send, swap_recv, list_send, list_recv, own_sem,
+    swap_send, swap_recv, list_send, list_recv, relay_ref, relay_send, relay_recv, own_sem,
 ):
     rows, cols, depths = sizes
     window = rows * depths
@@ -321,9 +320,15 @@
     r, c, d = position()
     me = r * depths + d
     diag = d // panels == c
-    parts = [(0, short)]
-    if capacity > short:
-        parts.append((short, capacity - short))
+    parts = [(0, short, 0)]
+    extra = capacity - short
+    ways = [1, 2] if cols == 4 and extra >= 4 else []
+    straight = extra // 4 if ways else extra
+    if extra:
+        parts.append((short, straight, 0))
+    if ways:
+        parts.append((short + straight, straight, 1))
+        parts.append((short + 2 * straight, extra - 2 * straight, 2))
 
     barrier = pltpu.get_barrier_semaphore()
 
@@ -335,6 +340,12 @@
     @pl.loop(1, cols)
     def _(off):
         pl.semaphore_signal(barrier, inc=1, device_id=(r, (c + off) % cols, d), device_id_type=MESH)
+
+    for way in ways:
+        @pl.loop(1, depths)
+        def _(off):
+            device = (r, c ^ way, (d + off) % depths)
+            pl.semaphore_signal(barrier, inc=1, device_id=device, device_id_type=MESH)
 
     own = [
         pltpu.make_async_copy(codes_ref.at[me], got_codes_ref.at[me], own_sem.at[0]),
@@ -342,7 +353,7 @@
     ]
     for copy in own:
         copy.start()
-    pl.semaphore_wait(barrier, window - 1 + cols - 1)
+    pl.semaphore_wait(barrier, window - 1 + cols - 1 + len(ways) * (depths - 1))
 
     def remote(src, dst, send, recv, device):
         return pltpu.make_async_remote_copy(
@@ -361,7 +372,7 @@
         )
 
     def swap_copy(part, depth):
-        first, length = parts[part]
+        first, length, way = parts[part]
         there = pl.ds(first, length)
         return remote(
             pack_ref.at[(1 - r) * depths + depth, there], merged_ref.at[depth, there],
@@ -375,34 +386,58 @@
         )
 
     def list_copy(part, slot, depth):
-        first, length = parts[part]
+        first, length, way = parts[part]
         there = pl.ds(first, length)
+        if way:
+            target, device = relay_ref.at[way - 1, depth, pl.ds(0, length)], (r, c ^ way, d)
+        else:
+            target, device = got_ref.at[slot, there], (r, c, depth)
         return remote(
-            merged_ref.at[depth, there], got_ref.at[slot, there],
-            list_send.at[part, depth], list_recv.at[part, slot], (r, c, depth),
-        )
+            merged_ref.at[depth, there], target,
+            list_send.at[part, depth], list_recv.at[part, depth if way else slot], device,
+        )
+
+    def relay_copy(part, slot, depth):
+        first, length, way = parts[part]
+        return remote(
+            relay_ref.at[way - 1, depth, pl.ds(0, length)],
+            got_ref.at[slot, pl.ds(first, length)],
+            relay_send.at[part, depth], relay_recv.at[part, slot], (r, c ^ way, depth),
+        )
+
+    def arrival(part, depth):
+        copy = relay_copy if parts[part][2] else list_copy
+        return copy(part, depth, depth)
 
     def each_part(wide, action):
-        action(0)
         if len(parts) > 1:
             @pl.when(wide)
             def _():
-                action(1)
+                for part in reversed(range(1, len(parts))):
+                    action(part)
+        action(0)
+
+    def each_relay(action):
+        for part, (first, length, way) in enumerate(parts):
+            if way:
+                @pl.when(d // panels == c ^ way)
+                def _():
+                    @pl.loop(1, depths)
+                    def _(off):
+                        action(part, (d + off) % depths)
 
     @pl.loop(1, depths)
     def _(off):
         depth = (d + off) % depths
         each_part(diag, lambda part: swap_copy(part, depth).start())
 
-    begin()
-
     @pl.loop(1, depths)
     def _(off):
         depth = (d + off) % depths
 
         def forward(part):
             swap_copy(part, depth).wait_recv()
-            first, length = parts[part]
+            first, length, way = parts[part]
             q = r * depths + depth
             count = jnp.broadcast_to(codes_ref[q, 0:1, 0:1], pack_ref.shape[2:])
             for place in range(first, first + length):
@@ -414,11 +449,18 @@
 
         each_part(diag, forward)
 
+    begin()
     chip_copy().start()
 
     @pl.loop(1, window)
     def _(off):
         code_copy(me, (me + off) % window).start()
+
+    def relay(part, depth):
+        list_copy(part, d, depth).wait_recv()
+        relay_copy(part, d, depth).start()
+
+    each_relay(relay)
 
     for copy in own:
         copy.wait()
@@ -438,8 +480,10 @@
     def _(off):
         depth = (d + off) % depths
         each_part(diag, lambda part: swap_copy(part, depth).wait_send())
-        each_part(depth // panels == c, lambda part: list_copy(part, depth, depth).wait_recv())
+        each_part(depth // panels == c, lambda part: arrival(part, depth).wait_recv())
         each_part(diag, lambda part: list_copy(part, d, depth).wait_send())
+
+    each_relay(lambda part, depth: relay_copy(part, d, depth).wait_send())
 
 
 def exchange(pack, codes, blocks, sizes, short, ident):
@@ -461,7 +505,9 @@
         scratch_shapes=[
             pltpu.VMEM(lists, jnp.float32),
             sem((window,)), sem((window,)), sem((2, max(3, cols))), sem((2, cols)),
-            sem((2, depths)), sem((2, depths)), sem((2, depths)), sem((2, depths)), sem((2,)),
+            sem((4, depths)), sem((4, depths)), sem((4, depths)), sem((4, depths)),
+            pltpu.VMEM((2, depths, max(1, (capacity - short) // 2), size, size), jnp.float32),
+            sem((4, depths)), sem((4, depths)), sem((2,)),
         ],
         compiler_params=pltpu.CompilerParams(
             collective_id=ident, has_side_effects=True, vmem_limit_bytes=VMEM_LIMIT
@@ -657,14 +703,23 @@
             got_codes, got, blocks, squares, (square,), block_shape, vmem,
         )
 
-    short = min(SHORT, most)
-    *lists, too_long = square_step(short, min(SHORT_DIAG, most), 1)
-
-    def again():
-        *lists, _ = square_step(most, most, 3)
-        return cube_step(most, *lists)
-
-    out = lax.cond(too_long[0, 0] != 0, again, lambda: cube_step(short, *lists))
+    sizes_tried = []
+    for short, capacity in TIERS:
+        tier = (min(short, most), min(capacity, most))
+        if tier not in sizes_tried:
+            sizes_tried.append(tier)
+    sizes_tried.append((most, most))
+
+    def attempt(tier):
+        short, capacity = sizes_tried[tier]
+        *lists, too_long = square_step(short, capacity, 1 + 2 * tier)
+        if (short, capacity) == (most, most):
+            return cube_step(short, *lists)
+        return lax.cond(
+            too_long[0, 0] != 0, lambda: attempt(tier + 1), lambda: cube_step(short, *lists)
+        )
+
+    out = attempt(0)
     return out[None]
 
 

time: 68.9 us -> 63 us (0.914)
  Pallas kernels: 64.9 us -> 60.3 us
  local copies, waits for them, and re-layouts: 2.74 us -> 2.04 us
    pallas_call x1, Pallas kernels: 30.4 us -> 24.1 us  [exchange(): pl.pallas_call(functools.partial(exchange_kernel, sizes, panels, short),...]
    pallas_call x1, Pallas kernels: 5.93 us -> 6.91 us  [pack_lists(): pl.pallas_call(functools.partial(pack_kernel, sizes, (local_rows, panels,...]
    unnamed x5 -> x3, local copies, waits for them, and re-layouts: 1.97 us -> 1.28 us
where the time goes in v6:
time: 63 us; the launch traced here: 63.3 us
  Pallas kernels  60.3 us (96%)
  local copies, waits for them, and re-layouts  2.04 us (3%)
  between operations  0.75 us (1%)
    pallas_call x1, Pallas kernels, exchange(): pl.pallas_call(functools.partial(exchange_kernel, sizes, panels, short),...  24.1 us
    pallas_call x1, Pallas kernels, gather_square(): pl.pallas_call(functools.partial(gather_kernel, cols), out_shape=(jax.Sha...  15.2 us
    pallas_call x1, Pallas kernels, gather_meta(): pl.pallas_call(functools.partial(meta_kernel, sizes, panels), out_shape=(...  9.71 us
    pallas_call x1, Pallas kernels, pack_lists(): pl.pallas_call(functools.partial(pack_kernel, sizes, (local_rows, panels,...  6.91 us
    pallas_call x2, Pallas kernels, local_product(): pl.pallas_call(kernel, out_shape=out_shape, in_specs=[pl.BlockSpec(memory...  4.41 us
    unnamed x3, local copies, waits for them, and re-layouts  1.28 us

profile of v6, /device:TPU:0, one launch (start us, length us, event | category | flops | bytes accessed | tf_op | source)
XLA Modules:
  0.0 63.3 jit_solution(6858555529996805641)
XLA Ops:
  0.0 0.8 %copy.11 = s32[64,1,4]{2,1,0:T(1,128)S(1)} copy(s32[64,1,4]{0,2,1:T(4,128)} %param.8) | data formatting | bytes 2048 | tf_op args[1]
  0.8 0.7 %copy.12 = s32[64,1,1]{2,1,0:T(1,128)S(1)} copy(s32[64,1,1]{0,2,1:T(1,128)} %bitcast.8) | data formatting | bytes 512 | tf_op jit(solution)/shard_map/broadcast_in_dim | solution.py:682
  1.5 0.1 pad_add_fusion
  1.7 9.7 %shard_map.39 = (s32[32,1,128]{2,1,0:T(1,128)S(1)}, s32[64,1,128]{2,1,0:T(1,128)S(1)}) custom-call(s32[64,1,128]{2,1,0:T(1,128)S(1)} %pad.4.local_ref), custom_call_target="tpu_custom_call" | custom-call | tf_op jit(solution)/shard_map/pallas_call | solution.py:185
  11.4 6.9 %shard_map.40 = (f32[8,6,128,128]{3,2,1,0:T(8,128)S(1)}, s32[8,1,128]{2,1,0:T(1,128)S(1)}) custom-call(s32[32,1,128]{2,1,0:T(1,128)S(1)} %get-tuple-element.95.win_ref, s32[64,1,128]{2,1,0:T(1,128)S(1)} %pad.4.local_ref, s32[64,1,128]{2,1,0:T(1,128)S(1)} %get-tuple-element.96.sibling_ref, f32[64,1,4,128,128]{4,3,2,1,0:T(8,128)} %blocks_ref.5), custom_call_target="tpu_custom_call" | custom-call | tf_op jit(solution)/shard_map/pallas_call | solution.py:297
  18.3 24.1 %shard_map.41 = (f32[4,6,128,128]{3,2,1,0:T(8,128)S(1)}, s32[8,1,128]{2,1,0:T(1,128)S(1)}, f32[4,1,4,128,128]{4,3,2,1,0:T(8,128)S(1)}) custom-call(f32[8,6,128,128]{3,2,1,0:T(8,128)S(1)} %get-tuple-element.97.pack_ref, s32[8,1,128]{2,1,0:T(1,128)S(1)} %get-tuple-element.98.codes_ref, f32[64,1,4,128,128]{4,3,2,1,0:T(8,128)} %blocks_ref.5), custom_call_target="tpu_custom_call" | custom-call | tf_op jit(solution)/shard_map/pallas_call | solution.py:496
  42.4 1.9 %shard_map.42 = (f32[1,4,128,128]{3,2,1,0:T(8,128)S(1)}, s32[1,128]{1,0:T(1,128)S(1)}) custom-call(s32[8,1,128]{2,1,0:T(1,128)S(1)} %get-tuple-element.99.codes_ref, f32[4,6,128,128]{3,2,1,0:T(8,128)S(1)} %get-tuple-element.100.got_ref, f32[64,1,4,128,128]{4,3,2,1,0:T(8,128)} %blocks_ref.5, f32[4,1,4,128,128]{4,3,2,1,0:T(8,128)S(1)} %get-tuple-element.101.lefts_ref), custom_call_target="tpu_custom_call" | custom-call | tf_op jit(solution)/shard_map/pallas_call | solution.py:586
  44.3 0.0 copy-start.5
  44.3 0.5 copy-done.5
  44.8 15.2 %shard_map.43 = (f32[4,1,4,128,128]{4,3,2,1,0:T(8,128)S(1)}, s32[1,128]{1,0:T(1,128)}) custom-call(f32[1,4,128,128]{3,2,1,0:T(8,128)S(1)} %get-tuple-element.102.square_ref, s32[1,128]{1,0:T(1,128)} %copy-done.5), custom_call_target="tpu_custom_call" | custom-call | tf_op jit(solution)/shard_map/pallas_call | solution.py:658
  60.7 2.6 %conditional.2 = ((f32[1,1,4,128,128]{4,3,2,1,0:T(8,128)})) conditional(s32[]{:T(128)} %bitcast.5, (s32[8,1,128]{2,1,0:T(1,128)S(1)}, f32[4,6,128,128]{3,2,1,0:T(8,128)S(1)}, f32[64,1,4,128,128]{4,3,2,1,0:T(8,128)}, f32[4,1,4,128,128]{4,3,2,1,0:T(8,128)S(1)}, f32[1,4,128,128]{3,2,1,0:T(8,128)S(1)}) %tuple.18, (s32[32,1,128]{2,1,0:T(1,128)S(1)}, ...), branch_computations={%region_0.1_spmd, %region_1.4_spmd} | conditional | flops 2 | bytes 39850248 | solution.py:718
  60.7 2.6 %branch_0_fun.2 = f32[1,4,128,128]{3,2,1,0:T(8,128)} custom-call(s32[8,1,128]{2,1,0:T(1,128)S(1)} %get-tuple-element.49.codes_ref, f32[4,6,128,128]{3,2,1,0:T(8,128)S(1)} %get-tuple-element.50.got_ref, f32[64,1,4,128,128]{4,3,2,1,0:T(8,128)} %get-tuple-element.51.blocks_ref, f32[4,1,4,128,128]{4,3,2,1,0:T(8,128)S(1)} %get-tuple-element.52.lefts_ref, ...), custom_call_target="tpu_custom_call" | custom-call | tf_op jit(solution)/shard_map/cond/branch_0_fun/pallas_call | solution.py:586
  (1 shorter events, 0.0 us)
Async XLA Ops:
  44.3 0.5 copy-start.5
